TPU v7x, 256 devices: a whole 4x4x8 slice. The times are simulated.
256 devices in a mesh: ctx: 16 (over x, y), fsdp: 16 (over z, core).
Axes of the slice: x: 4, y: 4, z: 8, core: 2. Of those that a mesh axis runs over, the one named last changes fastest.
Arguments:
- hidden: bfloat16 [16, 7168, 5120], P('fsdp', 'ctx'), may hold values from -6 to 6
- modulation: float32 [2, 5120], replicated, may hold values from -3 to 3
- head_weight: bfloat16 [64, 5120], replicated, may hold values from -0.078125 to 0.078125
- noisy: bfloat16 [16, 7168, 64], P('fsdp', 'ctx'), may hold values from -6 to 6
- timestep: int32 [1], replicated, may hold values from 1 to 999
- conv_weight: bfloat16 [3, 64, 384], replicated, may hold values from -0.4375 to 0.4375
- up_weight: bfloat16 [4, 384, 384], replicated, may hold values from -0.3125 to 0.3125
- patch_proj: bfloat16 [384, 1280], replicated, may hold values from -0.3125 to 0.3125
- fc1: bfloat16 [1280, 5120], P(None, 'fsdp'), may hold values from -0.15625 to 0.15625
- reward_vec: bfloat16 [1, 5120], P(None, 'fsdp'), may hold values from -0.078125 to 0.078125
Outputs:
- grad_hidden: bfloat16 [16, 7168, 5120], P('fsdp', 'ctx')
- rewards: float32 [16, 128], P('fsdp', 'ctx')
All inputs are finite; a program needn't handle non-finite values.
Results may differ from a plain program's by a relative error of at most 0.024.
Values may be sent and summed in bfloat16 or wider, within the bound.
A program may use at most 128 MiB of HBM per device.

v0:
```python
import jax
import jax.numpy as jnp
from jax import lax
from jax.sharding import PartitionSpec as P

DECODER_CHANNELS = 384
PATCH = 64
POOLED_REGIONS = 4
TPF = 224


LOSS_WEIGHT = 65536.0
EPSILON = 1e-06


def from_behind(x, axis, by):
    length = lax.axis_size(axis)
    pairs = [(i, i + by) for i in range(length) if 0 <= i + by < length]
    return lax.ppermute(x, axis, pairs)


def gelu_slope(value):
    coeff = 0.7978845608028654
    inner = coeff * (value + 0.044715 * value * value * value)
    tangent = jnp.tanh(inner)
    return 0.5 * (1.0 + tangent) + 0.5 * value * (1.0 - tangent * tangent) * coeff * (
        1.0 + 3.0 * 0.044715 * value * value
    )


def silu_slope(value):
    sig = jax.nn.sigmoid(value)
    return sig * (1.0 + value * (1.0 - sig))


def normalize(value):
    center = value - jnp.mean(value, axis=-1, keepdims=True)
    scale = lax.rsqrt(jnp.mean(center * center, axis=-1, keepdims=True) + EPSILON)
    return (center * scale, scale)


def norm_back(grad, normed, scale):
    return (
        grad
        - jnp.mean(grad, axis=-1, keepdims=True)
        - normed * jnp.mean(grad * normed, axis=-1, keepdims=True)
    ) * scale


def reward_terms(inputs, columns, readout):
    vec32 = readout[0].astype(jnp.float32)
    m = jnp.dot(inputs, columns, preferred_element_type=jnp.float32)
    reward_score = jnp.sum(jax.nn.gelu(m, approximate=True) * vec32, axis=-1)
    g = (vec32 * gelu_slope(m)).astype(jnp.bfloat16)
    back = lax.dot_general(g, columns, (((1,), (1,)), ((), ())), preferred_element_type=jnp.float32)
    return (reward_score, back)


def per_device(
    hidden,
    modulation,
    head_weight,
    noisy,
    timestep,
    conv_weight,
    up_weight,
    patch_proj,
    fc1,
    reward_vec,
):
    states = hidden[0]
    tokens = states.shape[0]
    frame_images = tokens // TPF
    frame_slot_count = frame_images * 4
    step_frac = timestep[0].astype(jnp.float32) / 1000.0
    sigma = 5.0 * step_frac / (1.0 + 4.0 * step_frac)
    normed, scale = normalize(states.astype(jnp.float32))
    modded = (normed * (1.0 + modulation[1]) + modulation[0]).astype(jnp.bfloat16)
    vel = lax.dot_general(
        modded, head_weight, (((1,), (1,)), ((), ())), preferred_element_type=jnp.float32
    )
    x0 = (
        (noisy[0].astype(jnp.float32) - sigma * vel)
        .astype(jnp.bfloat16)
        .reshape(frame_images, TPF, PATCH)
    )
    before = from_behind(x0, "ctx", 1)
    ext = jnp.concatenate([before, x0], axis=0)
    a0 = sum(
        (
            jnp.einsum(
                "ftp,pc->ftc",
                ext[2 - k : 2 - k + frame_images],
                conv_weight[k],
                preferred_element_type=jnp.float32,
            )
            for k in range(3)
        )
    )
    feat = jax.nn.silu(a0).astype(jnp.bfloat16)
    a1 = jnp.einsum("ftc,jcd->fjtd", feat, up_weight, preferred_element_type=jnp.float32)
    embedding_rows = jnp.mean(
        jax.nn.silu(a1).reshape(
            frame_images, 4, POOLED_REGIONS, TPF // POOLED_REGIONS, DECODER_CHANNELS
        ),
        axis=3,
    )
    embedding_rows = embedding_rows.astype(jnp.bfloat16).reshape(
        frame_slot_count * POOLED_REGIONS, DECODER_CHANNELS
    )
    slot_index = lax.axis_index("ctx") * frame_slot_count + jnp.arange(frame_slot_count)
    slot_present = ((slot_index == 0) | (slot_index >= 4)).astype(jnp.float32)
    u = jnp.dot(embedding_rows, patch_proj, preferred_element_type=jnp.float32)
    nhat, uscale = normalize(u)
    n = nhat.astype(jnp.bfloat16)
    columns = lax.all_gather(fc1, "fsdp", axis=1, tiled=True)
    readout = lax.all_gather(reward_vec, "fsdp", axis=1, tiled=True)
    reward_score, back = reward_terms(n, columns, readout)
    reward_score, dn = (reward_score, back)
    row_scale = jnp.repeat(-LOSS_WEIGHT * slot_present / POOLED_REGIONS, POOLED_REGIONS)
    dn = dn * row_scale[:, None]
    rewards = (
        jnp.mean(reward_score.reshape(frame_slot_count, POOLED_REGIONS), axis=1) * slot_present
    )
    du = norm_back(dn, nhat, uscale).astype(jnp.bfloat16)
    demb = lax.dot_general(
        du, patch_proj, (((1,), (1,)), ((), ())), preferred_element_type=jnp.float32
    )
    demb = demb.reshape(frame_images, 4, POOLED_REGIONS, 1, DECODER_CHANNELS)
    spread = jnp.broadcast_to(
        demb, (frame_images, 4, POOLED_REGIONS, TPF // POOLED_REGIONS, DECODER_CHANNELS)
    ).reshape(frame_images, 4, TPF, DECODER_CHANNELS)
    da1 = (spread / (TPF // POOLED_REGIONS) * silu_slope(a1)).astype(jnp.bfloat16)
    dfeat = jnp.einsum("fjtd,jcd->ftc", da1, up_weight, preferred_element_type=jnp.float32)
    da0 = (dfeat * silu_slope(a0)).astype(jnp.bfloat16)
    after = from_behind(da0, "ctx", -1)
    extd = jnp.concatenate([da0, after], axis=0)
    dx0 = sum(
        (
            jnp.einsum(
                "ftc,pc->ftp",
                extd[k : k + frame_images],
                conv_weight[k],
                preferred_element_type=jnp.float32,
            )
            for k in range(3)
        )
    )
    dvel = (-sigma * dx0).astype(jnp.bfloat16).reshape(tokens, PATCH)
    dmod = jnp.dot(dvel, head_weight, preferred_element_type=jnp.float32)
    dnormed = dmod * (1.0 + modulation[1])
    grad = norm_back(dnormed, normed, scale).astype(jnp.bfloat16)
    return (grad[None], rewards[None, :])


def solution(mesh):
    return jax.shard_map(
        per_device,
        mesh=mesh,
        in_specs=(
            P("fsdp", "ctx", None),
            P(),
            P(),
            P("fsdp", "ctx", None),
            P(),
            P(),
            P(),
            P(),
            P(None, "fsdp"),
            P(None, "fsdp"),
        ),
        out_specs=(P("fsdp", "ctx", None), P("fsdp", "ctx")),
        check_vma=False,
    )
```

profile of v0, /device:TPU:24, one launch (start us, length us, event | category | flops | bytes accessed | tf_op | source)
XLA Modules:
  0.0 140.4 jit_solution(9186543731235140739)
XLA Ops:
  7.2 0.0 copy-start
  7.2 0.0 all-gather.2.cloned.1.call-start
  7.2 0.7 all-gather.2.cloned.1.call-update
  7.9 0.0 copy-start.2
  8.8 0.0 copy-start.9
  8.8 0.0 copy-start.13
  8.8 0.0 copy-start.15
  8.8 3.4 %convert_reduce_fusion = f32[448]{0:T(512)S(1)} fusion(bf16[1,448,5120]{2,1,0:T(8,128)(2,1)} %param.10), kind=kLoop, calls=%fused_computation | loop fusion | flops 4587072 | bytes 4589312 | tf_op jit(solution)/shard_map/reduce_sum | solution.py:37
  12.2 0.0 copy-done.2
  12.2 1.3 fusion.12
  13.6 0.0 copy-done.9
  13.6 0.6 copy-done.7
  14.3 0.0 copy-start.16
  14.3 2.0 %fusion.36 = bf16[448,64]{0,1:T(8,128)(2,1)S(1)} fusion(bf16[64,5120]{1,0:T(8,128)(2,1)S(1)} %copy-done.13, bf16[1,448,5120]{2,1,0:T(8,128)(2,1)S(1)} %copy-done.2, f32[5120]{0:T(1024)S(1)} %bitcast.134, f32[5120]{0:T(1024)S(1)} %bitcast.131, f32[448]{0:T(512)S(1)} %add_rsqrt_fusion, f32[448]{0:T(512)S(1)} %broadcast_multiply_fusion.2, ...), kind=kOutput, calls=%fused_computation.42 | convolution fusion | flops 307478528 | bytes 5402116 | tf_op jit(solution)/shard_map/dot_general | solution.py:79
  16.3 0.1 reshape.108
  16.4 3.1 %collective-permute-start = (bf16[2,224,64]{1,2,0:T(8,128)(2,1)S(1)}, bf16[2,224,64]{1,2,0:T(8,128)(2,1)S(1)}, u32[]{:S(2)}, u32[]{:S(2)}) collective-permute-start(bf16[2,224,64]{1,2,0:T(8,128)(2,1)S(1)} %copy.15), channel_id=1, source_target_pairs={{0,16},{16,32},{32,48},{48,64},{64,80},{80,96},{96,112},{112,128},... | collective-permute-start | bytes 172040 | tf_op jit(solution)/shard_map/ppermute | solution.py:19
  19.5 0.0 copy-done.6
  19.5 0.3 fusion.87
  19.8 0.1 broadcast_in_dim.6
  19.9 0.7 mul.237
  20.6 0.0 copy-done.16
  20.6 0.6 dynamic-slice
  21.8 0.3 dynamic-update-slice
  22.1 54.7 %all-reduce = bf16[5120]{0:T(1024)(128)(2,1)S(1)} all-reduce(bf16[5120]{0:T(1024)(128)(2,1)S(1)} %dynamic-update-slice), channel_id=1, replica_groups=mesh['ctx'=16,'fsdp'=16] {'fsdp'}, use_global_device_ids=true, to_apply=%add | all-reduce | flops 5120 | bytes 20480
  76.8 0.6 mul.263
  77.4 0.0 collective-permute-done
  77.4 0.3 fusion.81
  77.7 0.3 fusion.22
  78.0 0.0 copy-done
  78.0 0.0 copy-start.4
  78.0 0.0 copy-start.3
  78.0 3.5 %bitcast_multiply_fusion.2 = (f32[2,4,224,384]{3,2,1,0:T(8,128)}, f32[2,224,4,384]{3,1,2,0:T(8,128)}) fusion(bf16[4,384,384]{2,1,0:T(8,128)(2,1)S(1)} %copy-done, f32[2,224,384]{2,1,0:T(8,128)S(1)} %fusion.22), kind=kOutput, calls=%fused_computation.21 | convolution fusion | flops 532094976 | bytes 7372800 | tf_op jit(solution)/shard_map/ftc,jcd->fjtd/dot_general | solution.py:101
  81.5 0.0 copy-done.4
  81.6 2.1 %reduce_sum.101 = f32[2,4,4,384]{3,2,1,0:T(4,128)S(1)} reduce(f32[2,4,4,56,384]{4,3,2,1,0:T(8,128)} %bitcast.130, f32[]{:T(128)} %constant.54.clone.1), dimensions={3}, to_apply=%region_2.3 | reduce | flops 675840 | bytes 2801668 | tf_op jit(solution)/shard_map/reduce_sum | solution.py:102
  83.7 0.4 fusion.106
  84.1 0.2 multiply_reduce_fusion.2
  84.3 0.5 add_rsqrt_fusion.1
  84.8 6.6 %all-gather.2.cloned.1.call-done = bf16[1280,5120]{0,1:T(8,128)(2,1)} async-done(((bf16[1280,320]{0,1:T(8,128)(2,1)}), bf16[1280,5120]{0,1:T(8,128)(2,1)}) %all-gather.2.cloned.1.call-update) | async-done | bytes 13107216 | tf_op jit(solution)/shard_map/all_gather | solution.py:116
  91.4 9.4 %fusion.58 = (f32[32]{0:T(128)}, f32[32,5120]{1,0:T(8,128)S(1)}) fusion(f32[5120]{0:T(1024)} %mul.263, bf16[1280,5120]{0,1:T(8,128)(2,1)} %all-gather.2.cloned.1.call-done, f32[32,1280]{1,0:T(8,128)S(1)} %get-tuple-element.11, f32[32]{0:T(128)} %add_rsqrt_fusion.1, f32[32]{0:T(128)S(1)} %broadcast_multiply_fusion.5), kind=kOutput, calls=%fused_computation.68 | convolution fusion | flops 421191648 | bytes 13947264 | tf_op jit(solution)/shard_map/dot_general | solution.py:52
  100.8 3.3 %fusion.105 = (f32[32]{0:T(128)S(1)}, f32[32]{0:T(128)S(1)}, f32[32,1280]{1,0:T(8,128)S(1)}) fusion(f32[32]{0:T(128)} %add_rsqrt_fusion.1, f32[32,1280]{1,0:T(8,128)S(1)} %get-tuple-element.11, f32[32]{0:T(128)S(1)} %broadcast_multiply_fusion.5, f32[32]{0:T(128)} %mul.237, bf16[1280,5120]{0,1:T(8,128)(2,1)S(1)} %copy-done.1, ...), kind=kOutput, calls=%fused_computation.129 | convolution fusion | flops 422789056 | bytes 14111360 | tf_op jit(solution)/shard_map/dot_general | solution.py:55
  104.1 0.0 copy-start.5
  104.1 0.4 convolution_multiply_fusion.1
  104.6 0.0 copy-start.11
  104.6 2.7 %fusion.16 = bf16[2,4,224,384]{3,2,1,0:T(8,128)(2,1)S(1)} fusion(f32[2,224,4,384]{3,1,2,0:T(8,128)} %get-tuple-element.9, f32[2,4,4,384]{3,2,1,0:T(4,128)S(1)} %div.80), kind=kLoop, calls=%fused_computation.19 | loop fusion | flops 6193152 | bytes 4177920 | tf_op jit(solution)/shard_map/convert_element_type | solution.py:133
  107.3 0.0 copy-start.14
  107.4 0.9 fusion.24
  108.3 2.7 %collective-permute-start.1 = (bf16[2,224,384]{2,1,0:T(8,128)(2,1)S(1)}, bf16[2,224,384]{2,1,0:T(8,128)(2,1)S(1)}, u32[]{:S(2)}, u32[]{:S(2)}) collective-permute-start(bf16[2,224,384]{2,1,0:T(8,128)(2,1)S(1)} %fusion.24), channel_id=1, source_target_pairs={{16,0},{32,16},{48,32},{64,48},{80,64},{96,80},{112,96},{128,112},... | collective-permute-start | bytes 1032200 | tf_op jit(solution)/shard_map/ppermute | solution.py:19
  111.1 0.1 reshape.111
  111.1 0.1 reduce_sum.109
  111.3 0.5 or_select_fusion
  111.8 0.3 fusion.85
  112.0 10.5 %collective-permute-done.1 = bf16[2,224,384]{2,1,0:T(8,128)(2,1)S(1)} collective-permute-done((bf16[2,224,384]{2,1,0:T(8,128)(2,1)S(1)}, bf16[2,224,384]{2,1,0:T(8,128)(2,1)S(1)}, u32[]{:S(2)}, u32[]{:S(2)}) %collective-permute-start.1) | collective-permute-done | bytes 344096 | tf_op jit(solution)/shard_map/ppermute | solution.py:19
  122.5 0.3 fusion.79
  122.8 0.0 slice-start
  122.8 0.3 fusion.39
  123.1 0.1 copy.18
  123.2 0.1 reshape.110
  123.3 0.0 copy-done.8
  123.3 0.0 copy-done.14
  123.3 0.0 slice-start.1
  123.3 4.8 %multiply_reduce_fusion = (f32[448]{0:T(512)S(1)}, f32[448]{0:T(512)S(1)}, f32[448,5120]{1,0:T(8,128)S(1)}) fusion(f32[5120]{0:T(1024)S(1)} %bitcast.132, f32[448]{0:T(512)S(1)} %add_rsqrt_fusion, f32[448]{0:T(512)S(1)} %broadcast_multiply_fusion.2, bf16[1,448,5120]{2,1,0:T(8,128)(2,1)} %param.10, bf16[448,64]{0,1:T(8,128)(2,1)S(1)} %reshape.110, ...), kind=kOutput, calls=%fused_computation.15 | convolution fusion | flops 309656704 | bytes 14502912 | tf_op jit(solution)/shard_map/dot_general | solution.py:150
  128.1 0.0 slice-done
  128.1 0.0 slice-done.1
  128.1 5.4 %fusion.13 = bf16[1,448,5120]{2,1,0:T(8,128)(2,1)} fusion(bf16[1,448,5120]{2,1,0:T(8,128)(2,1)S(1)} %bitcast.129, f32[448,5120]{1,0:T(8,128)S(1)} %get-tuple-element.13, f32[448]{0:T(512)S(1)} %broadcast_multiply_fusion, f32[448]{0:T(512)S(1)} %broadcast_multiply_fusion.1, f32[5120]{0:T(1024)S(1)} %bitcast.133, f32[448]{0:T(512)S(1)} %add_rsqrt_fusion, ...), kind=kLoop, calls=%fused_computation.16 | loop fusion | flops 20643840 | bytes 18377728 | tf_op jit(solution)/shard_map/broadcast_in_dim | solution.py:153
  (29 shorter events, 0.2 us)
Async XLA Ops:
  7.2 70.8 %copy-start = (bf16[4,384,384]{2,1,0:T(8,128)(2,1)S(1)}, bf16[4,384,384]{2,1,0:T(8,128)(2,1)}, u32[]{:S(2)}) copy-start(bf16[4,384,384]{2,1,0:T(8,128)(2,1)} %param.16) | copy-start | bytes 3538948
  7.2 84.2 %all-gather.2.cloned.1.call-start = ((), (), s32[]{:S(2)}) async-start(), calls=%async_computation | async-start | bytes 13926400 | tf_op jit(solution)/shard_map/all_gather | solution.py:116
  7.9 4.3 %copy-start.2 = (bf16[1,448,5120]{2,1,0:T(8,128)(2,1)S(1)}, bf16[1,448,5120]{2,1,0:T(8,128)(2,1)}, u32[]{:S(2)}) copy-start(bf16[1,448,5120]{2,1,0:T(8,128)(2,1)} %param.10) | copy-start | bytes 13762564
  8.8 4.8 %copy-start.9 = (f32[2,5120]{1,0:T(2,128)S(1)}, f32[2,5120]{1,0:T(2,128)}, u32[]{:S(2)}) copy-start(f32[2,5120]{1,0:T(2,128)} %param.11) | copy-start | bytes 122884
  8.8 5.5 %copy-start.13 = (bf16[64,5120]{1,0:T(8,128)(2,1)S(1)}, bf16[64,5120]{1,0:T(8,128)(2,1)}, u32[]{:S(2)}) copy-start(bf16[64,5120]{1,0:T(8,128)(2,1)} %param.12) | copy-start | bytes 1966084
  8.8 5.5 %copy-start.15 = (bf16[1,448,64]{1,2,0:T(8,128)(2,1)S(1)}, bf16[1,448,64]{1,2,0:T(8,128)(2,1)}, u32[]{:S(2)}) copy-start(bf16[1,448,64]{1,2,0:T(8,128)(2,1)} %param.13) | copy-start | bytes 172036
  13.6 0.6 copy-start.7
  14.2 5.2 %copy-start.6 = (bf16[3,64,384]{2,1,0:T(8,128)(2,1)S(1)}, bf16[3,64,384]{2,1,0:T(8,128)(2,1)}, u32[]{:S(2)}) copy-start(bf16[3,64,384]{2,1,0:T(8,128)(2,1)} %param.15) | copy-start | bytes 442372
  14.2 6.3 %copy-start.12 = (bf16[1,320]{1,0:T(2,128)(2,1)S(1)}, bf16[1,320]{1,0:T(2,128)(2,1)}, u32[]{:S(2)}) copy-start(bf16[1,320]{1,0:T(2,128)(2,1)} %param.19) | copy-start | bytes 1924
  14.3 6.3 %copy-start.16 = (u32[256]{0:T(256)S(1)}, u32[256]{0:T(256)}, u32[]{:S(2)}) copy-start(u32[256]{0:T(256)} %constant.75) | copy-start | bytes 3076
  16.4 61.0 %collective-permute-start = (bf16[2,224,64]{1,2,0:T(8,128)(2,1)S(1)}, bf16[2,224,64]{1,2,0:T(8,128)(2,1)S(1)}, u32[]{:S(2)}, u32[]{:S(2)}) collective-permute-start(bf16[2,224,64]{1,2,0:T(8,128)(2,1)S(1)} %copy.15), channel_id=1, source_target_pairs={{0,16},{16,32},{32,48},{48,64},{64,80},{80,96},{96,112},{112,128},... | collective-permute-start | bytes 172040 | tf_op jit(solution)/shard_map/ppermute | solution.py:19
  78.0 3.6 %copy-start.4 = (f32[2,224,384]{2,1,0:T(8,128)}, f32[2,224,384]{2,1,0:T(8,128)S(1)}, u32[]{:S(2)}) copy-start(f32[2,224,384]{2,1,0:T(8,128)S(1)} %fusion.22) | copy-start | bytes 2064388
  78.0 5.7 %copy-start.3 = (bf16[384,1280]{1,0:T(8,128)(2,1)S(1)}, bf16[384,1280]{1,0:T(8,128)(2,1)}, u32[]{:S(2)}) copy-start(bf16[384,1280]{1,0:T(8,128)(2,1)} %param.17) | copy-start | bytes 2949124
  91.4 9.4 %copy-start.1 = (bf16[1280,5120]{0,1:T(8,128)(2,1)S(1)}, bf16[1280,5120]{0,1:T(8,128)(2,1)}, u32[]{:S(2)}) copy-start(bf16[1280,5120]{0,1:T(8,128)(2,1)} %all-gather.2.cloned.1.call-done) | copy-start | bytes 39321604
  100.8 3.3 %copy-start.10 = (f32[32]{0:T(128)S(1)}, f32[32]{0:T(128)}, u32[]{:S(2)}) copy-start(f32[32]{0:T(128)} %add_rsqrt_fusion.1) | copy-start | bytes 388
  104.1 3.2 %copy-start.5 = (f32[2,224,384]{2,1,0:T(8,128)S(1)}, f32[2,224,384]{2,1,0:T(8,128)}, u32[]{:S(2)}) copy-start(f32[2,224,384]{2,1,0:T(8,128)} %copy-done.4) | copy-start | bytes 2064388
  104.6 6.5 %copy-start.11 = (f32[32]{0:T(128)S(1)}, f32[32]{0:T(128)}, u32[]{:S(2)}) copy-start(f32[32]{0:T(128)} %get-tuple-element.14) | copy-start | bytes 388
  107.3 15.9 %copy-start.8 = (f32[1,5120]{1,0:T(1,128)S(1)}, f32[1,5120]{1,0:T(1,128)}, u32[]{:S(2)}) copy-start(f32[1,5120]{1,0:T(1,128)} %copy-done.7) | copy-start | bytes 61444
  107.3 15.9 %copy-start.14 = (bf16[64,5120]{1,0:T(8,128)(2,1)S(1)}, bf16[64,5120]{1,0:T(8,128)(2,1)}, u32[]{:S(2)}) copy-start(bf16[64,5120]{1,0:T(8,128)(2,1)} %param.12) | copy-start | bytes 1966084
  108.3 14.2 %collective-permute-start.1 = (bf16[2,224,384]{2,1,0:T(8,128)(2,1)S(1)}, bf16[2,224,384]{2,1,0:T(8,128)(2,1)S(1)}, u32[]{:S(2)}, u32[]{:S(2)}) collective-permute-start(bf16[2,224,384]{2,1,0:T(8,128)(2,1)S(1)} %fusion.24), channel_id=1, source_target_pairs={{16,0},{32,16},{48,32},{64,48},{80,64},{96,80},{112,96},{128,112},... | collective-permute-start | bytes 1032200 | tf_op jit(solution)/shard_map/ppermute | solution.py:19
  122.8 5.3 %slice-start = ((s8[4587520]{0:T(1024)(128)(4,1)}), s8[393216]{0:T(1024)(128)(4,1)S(1)}, s32[]{:S(2)}) async-start(s8[4587520]{0:T(1024)(128)(4,1)} %bitcast.128), calls=%async_computation.1 | async-start | bytes 786432
  123.3 4.8 %slice-start.1 = ((s8[4587520]{0:T(1024)(128)(4,1)}), s8[4194304]{0:T(1024)(128)(4,1)S(1)}, s32[]{:S(2)}) async-start(s8[4587520]{0:T(1024)(128)(4,1)} %bitcast.128), calls=%async_computation.2 | async-start | bytes 8388608
Sparse Core Ops, SparseCore 0:
  9.8 81.5 all-gather.1
where the time goes:
time: 141 us; the launch traced here: 140 us
  blocking collectives  54.7 us (39%)
  matrix products  26.4 us (19%)
  waiting for transfers between devices  17.8 us (13%)
  other arithmetic  17 us (12%)
  between operations  16 us (11%)
  starting transfers between devices  5.84 us (4%)
  local copies, waits for them, and re-layouts  2.67 us (2%)
    unnamed x1, blocking collectives  54.7 us
    ppermute x2, waiting for transfers between devices, from_behind(): return lax.ppermute(x, axis, pairs)  10.5 us
    dot_general x1, matrix products, reward_terms(): m = jnp.dot(inputs, columns, preferred_element_type=jnp.float32)  9.42 us
    all_gather x1, waiting for transfers between devices, per_device(): columns = lax.all_gather(fc1, 'fsdp', axis=1, tiled=True)  6.59 us
    ppermute x2, starting transfers between devices, from_behind(): return lax.ppermute(x, axis, pairs)  5.81 us
    broadcast_in_dim x1, other arithmetic, per_device(): return (grad[None], rewards[None, :])  5.38 us
    dot_general x1, matrix products, per_device(): dmod = jnp.dot(dvel, head_weight, preferred_element_type=jnp.float32)  4.79 us
    dot_general x1, matrix products, per_device(): jnp.einsum('ftc,jcd->fjtd', feat, up_weight, preferred_element_type=jnp.f...  3.54 us
  transfers between devices with their start and end apart: 3, of which 2 were waited for; matrix products, arithmetic and copies ran while one was open for 13% of the time, Pallas kernels for 0%

commit v1 on v0

v1 whole, which is shorter than its diff:
```python
import jax
import jax.numpy as jnp
from jax import lax
from jax.experimental import pallas as pl
from jax.experimental.pallas import tpu as pltpu
from jax.sharding import PartitionSpec as P

TPF = 224
REGIONS = 4
SUB = 4
LOSS_WEIGHT = 65536.0
EPSILON = 1e-06
F32 = jnp.float32
BF16 = jnp.bfloat16
MESH = pl.DeviceIdType.MESH


def dot_nn(a, b):
    return lax.dot_general(a, b, (((1,), (0,)), ((), ())), preferred_element_type=F32)


def dot_nt(a, b):
    return lax.dot_general(a, b, (((1,), (1,)), ((), ())), preferred_element_type=F32)


def sigmoid(value):
    return 0.5 + 0.5 * jnp.tanh(0.5 * value)


def main_kernel(
    timestep,
    hidden,
    modulation,
    head_weight,
    noisy_t,
    conv_weight,
    up_weight,
    patch_proj,
    fc1_t,
    reward_vec,
    lhs_out,
    coef_out,
    reward_out,
    hid,
    mod,
    head,
    noisy,
    conv,
    up,
    proj,
    cols,
    vec,
    vec_in,
    acc,
    aux,
    ssq,
    pilot,
    vel0,
    rstd,
    mean,
    xown,
    xhalo,
    a0,
    feat,
    a1,
    emb32,
    eall,
    u,
    uscale,
    n,
    g,
    dn,
    du,
    dsend,
    drecv,
    ssend,
    srecv,
    da1,
    da0,
    hsend,
    hrecv,
    hid_sem,
    in_sem,
    far_send,
    far_recv,
    emb_send,
    emb_recv,
    dem_send,
    dem_recv,
    sco_send,
    sco_recv,
):
    chunks, tokens, width = hid.shape
    full = chunks * width
    patch = head.shape[0]
    channels = proj.shape[0]
    shard = fc1_t.shape[0]
    span = TPF // REGIONS
    rows = eall.shape[1]
    spots = eall.shape[0]

    ctx, fsdp = lax.axis_index("ctx"), lax.axis_index("fsdp")
    steps, flat = lax.axis_size("ctx"), lax.axis_size("fsdp")
    z, core = fsdp // 2, fsdp % 2
    after = (lax.rem(ctx + 1, steps), fsdp)
    before = (lax.rem(ctx + steps - 1, steps), fsdp)
    twin = (ctx, z * 2 + 1 - core)
    ups = [None] + [(ctx, lax.rem(z + d, spots) * 2 + core) for d in range(1, spots)]
    downs = [None] + [(ctx, lax.rem(z + spots - d, spots) * 2 + core) for d in range(1, spots)]

    loads = []

    def load(source, target):
        copy = pltpu.make_async_copy(source, target, in_sem.at[len(loads)])
        copy.start()
        loads.append(copy)
        return copy

    hid_loads = []

    def load_hidden(k):
        copy = pltpu.make_async_copy(
            hidden.at[:, pl.ds(k * width, width)], hid.at[k], hid_sem.at[k]
        )
        copy.start()
        hid_loads.append(copy)

    load_mod = load(modulation, mod)
    load_head = load(head_weight, head)
    for k in range(chunks):
        load_hidden(k)

    barrier = pltpu.get_barrier_semaphore()
    peers = [after, before, twin] + ups[1:]
    for peer in peers:
        pl.semaphore_signal(barrier, inc=1, device_id=peer, device_id_type=MESH)

    load_noisy = load(noisy_t, noisy)
    load_conv = []
    for frame in range(2):
        for lag in range(3):
            block = frame + 2 - lag
            load_conv.append(
                load(
                    conv_weight.at[lag],
                    conv.at[pl.ds(block * patch, patch), pl.ds(frame * channels, channels)],
                )
            )
    load_up = [
        load(up_weight.at[j], up.at[:, pl.ds(j * channels, channels)]) for j in range(SUB)
    ]
    load_proj = load(patch_proj, proj)
    load_cols = load(fc1_t, cols.at[pl.ds(0, shard)])
    load_vec = load(reward_vec, vec_in)

    empty = jnp.zeros((patch, channels), BF16)
    conv[0:patch, channels:] = empty
    conv[3 * patch :, :channels] = empty

    step_frac = jnp.full((1, 2 * patch), timestep[0].astype(F32)) / 1000.0
    sigma = 5.0 * step_frac / (1.0 + 4.0 * step_frac)
    left = lax.broadcasted_iota(jnp.int32, (TPF, 2 * patch), 1) < patch

    load_mod.wait()
    load_head.wait()
    hid_loads[0].wait()
    pilot[...] = jnp.broadcast_to(hid[0, :, 0:1].astype(F32), pilot.shape)
    acc[...] = jnp.zeros_like(acc)
    aux[...] = jnp.zeros_like(aux)
    ssq[...] = jnp.zeros_like(ssq)
    lanes = pilot.shape[1]
    block_rows = 16

    def features(k, carry):
        columns = pl.ds(pl.multiple_of(k * width, width), width)
        shift = mod[0:1, columns]
        high = shift.astype(BF16)
        low = (shift - high.astype(F32)).astype(BF16)
        side = jnp.concatenate(
            [
                jnp.ones((8, width), F32),
                jnp.broadcast_to(high.astype(F32), (8, width)),
                jnp.broadcast_to(low.astype(F32), (8, width)),
                jnp.zeros((8, width), F32),
            ],
            axis=0,
        ).astype(BF16)
        plain = head[:, columns]
        scaled = (plain.astype(F32) * (1.0 + mod[1:2, columns])).astype(BF16)
        ones = jnp.ones((patch, width), BF16)
        acc[...] += dot_nt(hid[k], jnp.concatenate([scaled, ones], axis=0))
        aux[...] += dot_nt(side, jnp.concatenate([scaled, plain], axis=0))
        for r in range(0, tokens, block_rows):
            centre = pilot[r : r + block_rows, :]
            total = ssq[r : r + block_rows, :]
            for c in range(0, width, lanes):
                value = hid[k, r : r + block_rows, c : c + lanes].astype(F32) - centre
                total = total + value * value
            ssq[r : r + block_rows, :] = total
        return carry

    features(0, 0)

    def later(k, carry):
        pltpu.make_async_copy(hid.at[k], hid.at[k], hid_sem.at[k]).wait()
        return features(k, carry)

    lax.fori_loop(1, chunks, later, 0)

    load_noisy.wait()
    pair = noisy[...]
    pair = jnp.concatenate([pair, pair], axis=0)
    row_id = lax.broadcasted_iota(jnp.int32, (TPF, 2 * TPF), 0)
    col_id = lax.broadcasted_iota(jnp.int32, (TPF, 2 * TPF), 1)
    first = dot_nt((row_id == col_id).astype(F32).astype(BF16), pair)
    second = dot_nt((row_id + TPF == col_id).astype(F32).astype(BF16), pair)
    latents = jnp.where(left, first, second)

    side_left = lax.broadcasted_iota(jnp.int32, (1, 2 * patch), 1) < patch
    sums = aux[0:1, :]
    shifts = aux[8:9, :] + aux[16:17, :]
    head_sums = jnp.where(side_left, sums, pltpu.roll(sums, patch, 1))
    head_shift = jnp.where(side_left, pltpu.roll(shifts, patch, 1), shifts)
    means, stds = [], []
    for f in range(2):
        part = slice(f * TPF, (f + 1) * TPF)
        average = acc[part, patch : patch + 1] / full
        off = average - pilot[part, 0:1]
        square = jnp.sum(ssq[part, :], axis=1, keepdims=True) / full
        var = jnp.maximum(square - off * off, 0.0)
        means.append(jnp.broadcast_to(average, (TPF, 2 * patch)))
        stds.append(jnp.broadcast_to(lax.rsqrt(var + EPSILON), (TPF, 2 * patch)))
    mean[...] = jnp.where(left, means[0], means[1])
    rstd[...] = jnp.where(left, stds[0], stds[1])
    product = jnp.where(left, acc[0:TPF, :], pltpu.roll(acc[TPF:, :], patch, 1))
    vel0[...] = rstd[...] * (product - mean[...] * head_sums)
    xown[...] = (latents - sigma * (vel0[...] + head_shift)).astype(BF16)

    pl.semaphore_wait(barrier, len(peers))

    def far(source, target, index, device):
        copy = pltpu.make_async_remote_copy(
            src_ref=source,
            dst_ref=target,
            send_sem=far_send.at[index],
            recv_sem=far_recv.at[index],
            device_id=device,
            device_id_type=MESH,
        )
        copy.start()
        return copy

    move_x = far(xown, xhalo, 0, after)
    move_cols = far(fc1_t, cols.at[pl.ds(shard, shard)], 1, twin)
    load_vec.wait()
    vec[0] = jnp.broadcast_to(vec_in[...].astype(F32), vec.shape[1:])
    move_vec = far(vec.at[0], vec.at[1], 2, twin)

    for copy in load_conv:
        copy.wait()
    a0[...] = dot_nn(xown[...], conv[2 * patch :, :])
    for copy in load_up:
        copy.wait()
    move_x.wait_recv()
    live_before = jnp.where(ctx > 0, 1.0, 0.0)
    halo = (xhalo[...].astype(F32) * live_before).astype(BF16)
    a0[...] += dot_nn(halo, conv[0 : 2 * patch, :])
    for f in range(2):
        value = a0[:, f * channels : (f + 1) * channels]
        feat[f * TPF : (f + 1) * TPF, :] = (value * sigmoid(value)).astype(BF16)

    for j in range(SUB):
        part = slice(j * channels, (j + 1) * channels)
        a1[:, part] = dot_nn(feat[...], up[:, part])
        for f in range(2):
            for p in range(REGIONS):
                begin = f * TPF + p * span
                value = a1[begin : begin + span, part]
                pooled = jnp.sum(value * sigmoid(value), axis=0, keepdims=True) / span
                row = p * 2 * SUB + f * SUB + j
                emb32[row : row + 1, :] = pooled
    eall[0] = emb32[...].astype(BF16)

    order = sorted(range(1, spots), key=lambda d: (-min(d, spots - d), d))
    move_emb = []
    for d in order:
        copy = pltpu.make_async_remote_copy(
            src_ref=eall.at[0],
            dst_ref=eall.at[d],
            send_sem=emb_send.at[d],
            recv_sem=emb_recv.at[d],
            device_id=ups[d],
            device_id_type=MESH,
        )
        copy.start()
        move_emb.append(copy)

    for f in range(2):
        for p in range(REGIONS):
            begin = f * TPF + p * span
            for j in range(SUB):
                part = slice(j * channels, (j + 1) * channels)
                value = a1[begin : begin + span, part]
                gate = sigmoid(value)
                a1[begin : begin + span, part] = gate * (1.0 + value * (1.0 - gate))
        part = slice(f * channels, (f + 1) * channels)
        value = a0[:, part]
        gate = sigmoid(value)
        a0[:, part] = gate * (1.0 + value * (1.0 - gate))

    load_proj.wait()
    load_cols.wait()
    move_cols.wait_recv()
    move_vec.wait_recv()
    for copy in move_emb:
        copy.wait_recv()

    features_r = proj.shape[1]
    stacked = jnp.concatenate([eall[d] for d in range(spots)], axis=0)
    u[...] = dot_nn(stacked, proj[...])
    for d in range(spots):
        part = slice(d * rows, (d + 1) * rows)
        value = u[part, :]
        centre = value - jnp.mean(value, axis=-1, keepdims=True)
        scale = lax.rsqrt(jnp.mean(centre * centre, axis=-1, keepdims=True) + EPSILON)
        normed = centre * scale
        u[part, :] = normed
        uscale[part, :] = jnp.broadcast_to(scale, (rows, uscale.shape[1]))
        n[part, :] = normed.astype(BF16)
    weight = jnp.concatenate([vec[0], vec[1]], axis=1)[0:1, :]
    coeff = 0.7978845608028654
    dn[:, : 2 * shard] = dot_nt(n[...], cols[...])
    for d in range(spots):
        part = slice(d * rows, (d + 1) * rows)
        value = dn[part, : 2 * shard]
        square = value * value
        tangent = jnp.tanh(coeff * (value + 0.044715 * value * square))
        half = 0.5 * (1.0 + tangent)
        slope = half + 0.5 * value * (1.0 - tangent * tangent) * (
            coeff * (1.0 + 3.0 * 0.044715 * square)
        )
        g[part, :] = (weight * slope).astype(BF16)
        score = value * half * weight
        slots = rows // REGIONS
        folded = score[0:slots]
        for p in range(1, REGIONS):
            folded = folded + score[p * slots : (p + 1) * slots]
        ssend[d] = jnp.broadcast_to(jnp.sum(folded, axis=1, keepdims=True), ssend.shape[1:])
    dn[...] = dot_nn(g[...], cols[...])
    slot = lax.rem(lax.broadcasted_iota(jnp.int32, (rows, 1), 0), rows // REGIONS) + ctx * (
        2 * SUB
    )
    present = jnp.where((slot == 0) | (slot >= SUB), 1.0, 0.0)
    row_scale = present * (-LOSS_WEIGHT / REGIONS / span)
    for d in range(spots):
        part = slice(d * rows, (d + 1) * rows)
        value = dn[part, :]
        normed = u[part, :]
        first = jnp.mean(value, axis=-1, keepdims=True)
        second = jnp.mean(value * normed, axis=-1, keepdims=True)
        du[part, :] = (
            (value - first - normed * second) * (uscale[part, 0:1] * row_scale)
        ).astype(BF16)
    back = dot_nt(du[...], proj[...])
    for d in range(spots):
        dsend[d] = back[d * rows : (d + 1) * rows].astype(BF16)

    move_dem, move_sco = [], []
    for d in order:
        copy = pltpu.make_async_remote_copy(
            src_ref=dsend.at[d],
            dst_ref=drecv.at[d],
            send_sem=dem_send.at[d],
            recv_sem=dem_recv.at[d],
            device_id=downs[d],
            device_id_type=MESH,
        )
        copy.start()
        move_dem.append(copy)
    for d in order:
        copy = pltpu.make_async_remote_copy(
            src_ref=ssend.at[d],
            dst_ref=srecv.at[d],
            send_sem=sco_send.at[d],
            recv_sem=sco_recv.at[d],
            device_id=downs[d],
            device_id_type=MESH,
        )
        copy.start()
        move_sco.append(copy)

    demb = back[0:rows]
    for copy in move_dem:
        copy.wait_recv()
    for d in range(1, spots):
        demb = demb + drecv[d].astype(F32)
    emb32[...] = demb

    for f in range(2):
        for j in range(SUB):
            part = slice(j * channels, (j + 1) * channels)
            spread = jnp.concatenate(
                [
                    jnp.broadcast_to(
                        emb32[p * 2 * SUB + f * SUB + j : p * 2 * SUB + f * SUB + j + 1, :],
                        (span, channels),
                    )
                    for p in range(REGIONS)
                ],
                axis=0,
            )
            da1[f * TPF : (f + 1) * TPF, part] = (
                spread * a1[f * TPF : (f + 1) * TPF, part]
            ).astype(BF16)
        dfeat = dot_nt(da1[f * TPF : (f + 1) * TPF, :], up[...])
        part = slice(f * channels, (f + 1) * channels)
        da0[:, part] = (dfeat * a0[:, part]).astype(BF16)
    hsend[...] = dot_nt(da0[...], conv[0 : 2 * patch, :]).astype(BF16)
    move_h = far(hsend, hrecv, 3, before)
    own = dot_nt(da0[...], conv[2 * patch :, :])

    total = ssend[0]
    for copy in move_sco:
        copy.wait_recv()
    for d in range(1, spots):
        total = total + srecv[d]
    slots = total.shape[0]
    index = lax.broadcasted_iota(jnp.int32, total.shape, 0)
    lane = lax.broadcasted_iota(jnp.int32, total.shape, 1)
    where = index + ctx * slots
    total = jnp.where((where == 0) | (where >= SUB), total / REGIONS, 0.0)
    reward_out[...] = jnp.sum(jnp.where(index == lane, total, 0.0), axis=0, keepdims=True)

    move_h.wait_recv()
    live_after = jnp.where(ctx < steps - 1, 1.0, 0.0)
    grad = (-sigma) * (own + hrecv[...].astype(F32) * live_after)
    lean = (rstd[...] * grad).astype(BF16).astype(F32)
    one = lean * head_sums
    two = lean * vel0[...]
    place = lax.broadcasted_iota(jnp.int32, (TPF, 2 * patch), 1)
    for f in range(2):
        mine = left if f == 0 else jnp.logical_not(left)
        spot = 0 if f == 0 else patch
        mean_one = jnp.sum(jnp.where(mine, one, 0.0), axis=1, keepdims=True) / full
        mean_two = jnp.sum(jnp.where(mine, two, 0.0), axis=1, keepdims=True) / full
        slope = rstd[:, spot : spot + 1] * mean_two
        offset = slope * mean[:, spot : spot + 1] - mean_one
        high = offset.astype(BF16).astype(F32)
        middle = (offset - high).astype(BF16).astype(F32)
        low = offset - high - middle
        tail = jnp.where(
            place == patch,
            high,
            jnp.where(place == patch + 1, middle, jnp.where(place == patch + 2, low, 0.0)),
        )
        body = lean if f == 0 else pltpu.roll(lean, patch, 1)
        lhs_out[f * TPF : (f + 1) * TPF, :] = jnp.where(left, body, tail).astype(BF16)
        coef_out[f * TPF : (f + 1) * TPF, :] = jnp.broadcast_to(slope, (TPF, 2 * patch))

    for copy in [move_x, move_cols, move_vec, move_h] + move_emb + move_dem + move_sco:
        copy.wait_send()


def tail_kernel(hidden, modulation, head_weight, lhs, coef, rewards, grad, reward_out):
    patch, width = head_weight.shape
    scaled = (head_weight[...].astype(F32) * (1.0 + modulation[1:2, :])).astype(BF16)
    weight = jnp.concatenate([scaled, jnp.ones((patch, width), BF16)], axis=0)
    lanes = coef.shape[1]
    block = 16
    product = dot_nn(lhs[...], weight)
    for r in range(0, hidden.shape[0], block):
        slope = coef[r : r + block, :]
        for c in range(0, width, lanes):
            value = hidden[r : r + block, c : c + lanes].astype(F32)
            grad[r : r + block, c : c + lanes] = (
                product[r : r + block, c : c + lanes] - value * slope
            ).astype(BF16)
    reward_out[...] = rewards[:, : reward_out.shape[1]]


def per_device(
    hidden,
    modulation,
    head_weight,
    noisy,
    timestep,
    conv_weight,
    up_weight,
    patch_proj,
    fc1,
    reward_vec,
):
    states = hidden[0]
    tokens, full = states.shape
    patch = head_weight.shape[0]
    channels = up_weight.shape[1]
    features_r, shard = fc1.shape
    spots = lax.axis_size("fsdp") // 2
    rows = 2 * SUB * REGIONS
    slots = 2 * SUB
    lanes = 2 * patch
    width = 512
    chunks = full // width
    wide = max(features_r, 2 * shard)

    def vmem(shape, dtype):
        return pltpu.VMEM(shape, dtype)

    scratch = [
        vmem((chunks, tokens, width), BF16),
        vmem((2, full), F32),
        vmem((patch, full), BF16),
        vmem((patch, tokens), BF16),
        vmem((4 * patch, 2 * channels), BF16),
        vmem((channels, SUB * channels), BF16),
        vmem((channels, features_r), BF16),
        vmem((2 * shard, features_r), BF16),
        vmem((2, 8, shard), F32),
        vmem((1, shard), BF16),
        vmem((tokens, lanes), F32),
        vmem((32, lanes), F32),
        vmem((tokens, lanes), F32),
        vmem((tokens, lanes), F32),
        vmem((TPF, lanes), F32),
        vmem((TPF, lanes), F32),
        vmem((TPF, lanes), F32),
        vmem((TPF, lanes), BF16),
        vmem((TPF, lanes), BF16),
        vmem((TPF, 2 * channels), F32),
        vmem((tokens, channels), BF16),
        vmem((tokens, SUB * channels), F32),
        vmem((rows, channels), F32),
        vmem((spots, rows, channels), BF16),
        vmem((spots * rows, features_r), F32),
        vmem((spots * rows, 128), F32),
        vmem((spots * rows, features_r), BF16),
        vmem((spots * rows, 2 * shard), BF16),
        vmem((spots * rows, wide), F32),
        vmem((spots * rows, features_r), BF16),
        vmem((spots, rows, channels), BF16),
        vmem((spots, rows, channels), BF16),
        vmem((spots, slots, 128), F32),
        vmem((spots, slots, 128), F32),
        vmem((tokens, SUB * channels), BF16),
        vmem((TPF, 2 * channels), BF16),
        vmem((TPF, lanes), BF16),
        vmem((TPF, lanes), BF16),
        pltpu.SemaphoreType.DMA((chunks,)),
        pltpu.SemaphoreType.DMA((16,)),
        pltpu.SemaphoreType.DMA((4,)),
        pltpu.SemaphoreType.DMA((4,)),
        pltpu.SemaphoreType.DMA((spots,)),
        pltpu.SemaphoreType.DMA((spots,)),
        pltpu.SemaphoreType.DMA((spots,)),
        pltpu.SemaphoreType.DMA((spots,)),
        pltpu.SemaphoreType.DMA((spots,)),
        pltpu.SemaphoreType.DMA((spots,)),
    ]
    anywhere = pl.BlockSpec(memory_space=pl.ANY)
    local = pl.BlockSpec(memory_space=pltpu.VMEM)
    lhs, coef, rewards = pl.pallas_call(
        main_kernel,
        out_shape=(
            jax.ShapeDtypeStruct((tokens, lanes), BF16),
            jax.ShapeDtypeStruct((tokens, lanes), F32),
            jax.ShapeDtypeStruct((1, 128), F32),
        ),
        in_specs=[pl.BlockSpec(memory_space=pltpu.SMEM)] + [anywhere] * 9,
        out_specs=(local, local, local),
        scratch_shapes=scratch,
        compiler_params=pltpu.CompilerParams(
            collective_id=0, has_side_effects=True, vmem_limit_bytes=36 * 1024 * 1024
        ),
        name="reward_step",
    )(
        timestep,
        states,
        modulation,
        head_weight,
        noisy[0].T,
        conv_weight,
        up_weight,
        patch_proj,
        fc1.T,
        reward_vec,
    )
    piece = 512
    grad, reward = pl.pallas_call(
        tail_kernel,
        grid=(full // piece,),
        out_shape=(
            jax.ShapeDtypeStruct((tokens, full), BF16),
            jax.ShapeDtypeStruct((1, slots), F32),
        ),
        in_specs=[
            pl.BlockSpec((tokens, piece), lambda i: (0, i)),
            pl.BlockSpec((2, piece), lambda i: (0, i)),
            pl.BlockSpec((patch, piece), lambda i: (0, i)),
            pl.BlockSpec((tokens, lanes), lambda i: (0, 0)),
            pl.BlockSpec((tokens, lanes), lambda i: (0, 0)),
            pl.BlockSpec((1, 128), lambda i: (0, 0)),
        ],
        out_specs=(
            pl.BlockSpec((tokens, piece), lambda i: (0, i)),
            pl.BlockSpec((1, slots), lambda i: (0, 0)),
        ),
        compiler_params=pltpu.CompilerParams(vmem_limit_bytes=16 * 1024 * 1024),
        name="hidden_gradient",
    )(states, modulation, head_weight, lhs, coef, rewards)
    return (grad[None], reward)


def solution(mesh):
    return jax.shard_map(
        per_device,
        mesh=mesh,
        in_specs=(
            P("fsdp", "ctx", None),
            P(),
            P(),
            P("fsdp", "ctx", None),
            P(),
            P(),
            P(),
            P(),
            P(None, "fsdp"),
            P(None, "fsdp"),
        ),
        out_specs=(P("fsdp", "ctx", None), P("fsdp", "ctx")),
        check_vma=False,
    )
```

time: 141 us -> 55.4 us (0.39)
  the two profiles are of different devices: /device:TPU:24 before, /device:TPU:30 now
where the time goes in v1:
time: 55.4 us; the launch traced here: 54.9 us
  Pallas kernels  43.4 us (78%)
  local copies, waits for them, and re-layouts  10.2 us (18%)
  between operations  1.3 us (2%)
    pallas_call x1, Pallas kernels, per_device(): pl.pallas_call(main_kernel, out_shape=(jax.ShapeDtypeStruct((tokens, lane...  37.7 us
    unnamed x18, local copies, waits for them, and re-layouts  10.2 us
    pallas_call x1, Pallas kernels, per_device(): pl.pallas_call(tail_kernel, grid=(full // piece,), out_shape=(jax.ShapeDt...  5.75 us

profile of v1, /device:TPU:30, one launch (start us, length us, event | category | flops | bytes accessed | tf_op | source)
XLA Modules:
  0.0 54.9 jit_solution(2981897619661806574)
XLA Ops:
  1.3 0.0 copy-start
  1.3 2.3 %copy-done = bf16[1,448,5120]{2,1,0:T(8,128)(2,1)S(1)} copy-done((bf16[1,448,5120]{2,1,0:T(8,128)(2,1)S(1)}, bf16[1,448,5120]{2,1,0:T(8,128)(2,1)}, u32[]{:S(2)}) %copy-start) | copy-done | bytes 4587544
  3.6 0.0 copy-start.1
  3.6 1.1 %copy-done.1 = bf16[64,5120]{1,0:T(8,128)(2,1)S(1)} copy-done((bf16[64,5120]{1,0:T(8,128)(2,1)S(1)}, bf16[64,5120]{1,0:T(8,128)(2,1)}, u32[]{:S(2)}) %copy-start.1) | copy-done | bytes 655384
  4.7 0.0 copy-start.2
  4.7 1.3 %copy-done.2 = bf16[4,384,384]{2,1,0:T(8,128)(2,1)S(1)} copy-done((bf16[4,384,384]{2,1,0:T(8,128)(2,1)S(1)}, bf16[4,384,384]{2,1,0:T(8,128)(2,1)}, u32[]{:S(2)}) %copy-start.2) | copy-done | bytes 1179672
  5.9 0.0 copy-start.3
  5.9 1.2 %copy-done.3 = bf16[384,1280]{1,0:T(8,128)(2,1)S(1)} copy-done((bf16[384,1280]{1,0:T(8,128)(2,1)S(1)}, bf16[384,1280]{1,0:T(8,128)(2,1)}, u32[]{:S(2)}) %copy-start.3) | copy-done | bytes 983064
  7.1 0.0 copy-start.4
  7.1 1.1 %copy-done.4 = bf16[1280,320]{0,1:T(8,128)(2,1)S(1)} copy-done((bf16[1280,320]{0,1:T(8,128)(2,1)S(1)}, bf16[1280,320]{0,1:T(8,128)(2,1)}, u32[]{:S(2)}) %copy-start.4) | copy-done | bytes 819224
  8.3 0.0 copy-start.5
  8.3 0.8 %copy-done.5 = f32[2,5120]{1,0:T(2,128)S(1)} copy-done((f32[2,5120]{1,0:T(2,128)S(1)}, f32[2,5120]{1,0:T(2,128)}, u32[]{:S(2)}) %copy-start.5) | copy-done | bytes 40984
  9.1 0.0 copy-start.6
  9.1 0.9 %copy-done.6 = bf16[3,64,384]{2,1,0:T(8,128)(2,1)S(1)} copy-done((bf16[3,64,384]{2,1,0:T(8,128)(2,1)S(1)}, bf16[3,64,384]{2,1,0:T(8,128)(2,1)}, u32[]{:S(2)}) %copy-start.6) | copy-done | bytes 147480
  10.0 0.0 copy-start.7
  10.0 0.8 %copy-done.7 = bf16[1,448,64]{1,2,0:T(8,128)(2,1)S(1)} copy-done((bf16[1,448,64]{1,2,0:T(8,128)(2,1)S(1)}, bf16[1,448,64]{1,2,0:T(8,128)(2,1)}, u32[]{:S(2)}) %copy-start.7) | copy-done | bytes 57368
  10.8 0.0 copy-start.8
  10.8 0.7 %copy-done.8 = bf16[1,320]{1,0:T(2,128)(2,1)S(1)} copy-done((bf16[1,320]{1,0:T(2,128)(2,1)S(1)}, bf16[1,320]{1,0:T(2,128)(2,1)}, u32[]{:S(2)}) %copy-start.8) | copy-done | bytes 664
  11.5 37.7 %reward_step.1 = (bf16[448,128]{1,0:T(8,128)(2,1)S(1)}, f32[448,128]{1,0:T(8,128)S(1)}, f32[1,128]{1,0:T(1,128)S(1)}) custom-call(s32[1]{0:T(128)S(6)} %copy.12.timestep, bf16[448,5120]{1,0:T(8,128)(2,1)S(1)} %bitcast.6, f32[2,5120]{1,0:T(2,128)S(1)} %copy-done.5, bf16[64,5120]{1,0:T(8,128)(2,1)S(1)} %copy-done.1, bf16[64,448]{1,0:T(8,128)(2,1)S(1)} %bitcast.9, ...), custom_call_target="tpu_custom_call" | custom-call | tf_op jit(solution)/shard_map/reward_step/pallas_call | solution.py:561
  49.2 5.8 %hidden_gradient.1 = (bf16[448,5120]{1,0:T(8,128)(2,1)}, f32[1,8]{1,0:T(1,128)}) custom-call(bf16[448,5120]{1,0:T(8,128)(2,1)S(1)} %bitcast.7, f32[2,5120]{1,0:T(2,128)S(1)} %copy-done.5, bf16[64,5120]{1,0:T(8,128)(2,1)S(1)} %copy-done.1, bf16[448,128]{1,0:T(8,128)(2,1)S(1)} %get-tuple-element.7.lhs, f32[448,128]{1,0:T(8,128)S(1)} %get-tuple-element.8.coef, ...), custom_call_target="tpu_custom_call" | custom-call | tf_op jit(solution)/shard_map/hidden_gradient/pallas_call | solution.py:588
Async XLA Ops:
  1.3 2.3 %copy-start = (bf16[1,448,5120]{2,1,0:T(8,128)(2,1)S(1)}, bf16[1,448,5120]{2,1,0:T(8,128)(2,1)}, u32[]{:S(2)}) copy-start(bf16[1,448,5120]{2,1,0:T(8,128)(2,1)} %param.10) | copy-start | bytes 13762564
  3.6 1.1 %copy-start.1 = (bf16[64,5120]{1,0:T(8,128)(2,1)S(1)}, bf16[64,5120]{1,0:T(8,128)(2,1)}, u32[]{:S(2)}) copy-start(bf16[64,5120]{1,0:T(8,128)(2,1)} %head_weight.3) | copy-start | bytes 1966084
  4.7 1.3 %copy-start.2 = (bf16[4,384,384]{2,1,0:T(8,128)(2,1)S(1)}, bf16[4,384,384]{2,1,0:T(8,128)(2,1)}, u32[]{:S(2)}) copy-start(bf16[4,384,384]{2,1,0:T(8,128)(2,1)} %up_weight.1) | copy-start | bytes 3538948
  5.9 1.2 %copy-start.3 = (bf16[384,1280]{1,0:T(8,128)(2,1)S(1)}, bf16[384,1280]{1,0:T(8,128)(2,1)}, u32[]{:S(2)}) copy-start(bf16[384,1280]{1,0:T(8,128)(2,1)} %patch_proj.1) | copy-start | bytes 2949124
  7.1 1.1 %copy-start.4 = (bf16[1280,320]{0,1:T(8,128)(2,1)S(1)}, bf16[1280,320]{0,1:T(8,128)(2,1)}, u32[]{:S(2)}) copy-start(bf16[1280,320]{0,1:T(8,128)(2,1)} %param.18) | copy-start | bytes 2457604
  8.3 0.8 %copy-start.5 = (f32[2,5120]{1,0:T(2,128)S(1)}, f32[2,5120]{1,0:T(2,128)}, u32[]{:S(2)}) copy-start(f32[2,5120]{1,0:T(2,128)} %modulation.3) | copy-start | bytes 122884
  9.1 0.9 %copy-start.6 = (bf16[3,64,384]{2,1,0:T(8,128)(2,1)S(1)}, bf16[3,64,384]{2,1,0:T(8,128)(2,1)}, u32[]{:S(2)}) copy-start(bf16[3,64,384]{2,1,0:T(8,128)(2,1)} %conv_weight.1) | copy-start | bytes 442372
  10.0 0.8 %copy-start.7 = (bf16[1,448,64]{1,2,0:T(8,128)(2,1)S(1)}, bf16[1,448,64]{1,2,0:T(8,128)(2,1)}, u32[]{:S(2)}) copy-start(bf16[1,448,64]{1,2,0:T(8,128)(2,1)} %param.13) | copy-start | bytes 172036
  10.8 0.7 %copy-start.8 = (bf16[1,320]{1,0:T(2,128)(2,1)S(1)}, bf16[1,320]{1,0:T(2,128)(2,1)}, u32[]{:S(2)}) copy-start(bf16[1,320]{1,0:T(2,128)(2,1)} %reward_vec.1) | copy-start | bytes 1924

commit v2 on v0

v2 whole, which is shorter than its diff:
```python
import jax
import jax.numpy as jnp
from jax import lax
from jax.experimental import pallas as pl
from jax.experimental.pallas import tpu as pltpu
from jax.sharding import PartitionSpec as P

TPF = 224
REGIONS = 4
SUB = 4
LOSS_WEIGHT = 65536.0
EPSILON = 1e-06
F32 = jnp.float32
BF16 = jnp.bfloat16
MESH = pl.DeviceIdType.MESH


def dot_nn(a, b):
    return lax.dot_general(a, b, (((1,), (0,)), ((), ())), preferred_element_type=F32)


def dot_nt(a, b):
    return lax.dot_general(a, b, (((1,), (1,)), ((), ())), preferred_element_type=F32)


def sigmoid(value):
    return 0.5 + 0.5 * jnp.tanh(0.5 * value)


def silu(value):
    half = 0.5 * value
    return half + half * jnp.tanh(half)


def silu_slope(value):
    half = 0.5 * value
    tangent = jnp.tanh(half)
    return (0.5 + 0.5 * tangent) * (1.0 + half * (1.0 - tangent))


def lane_sums(value, pattern):
    high = value.astype(BF16)
    low = (value - high.astype(F32)).astype(BF16)
    return dot_nn(high, pattern) + dot_nn(low, pattern)


def main_kernel(
    timestep_in,
    hidden,
    modulation,
    head_weight,
    noisy_t,
    conv_weight,
    up_weight,
    patch_proj,
    fc1_t,
    reward_vec,
    hid,
    wide,
    lhs_out,
    coef_out,
    reward_out,
    timestep,
    mod,
    head,
    noisy,
    conv,
    up,
    proj,
    cols,
    mixed,
    vec,
    vec_in,
    acc,
    ssq,
    pilot,
    sums_part,
    shift_part,
    latents,
    vel0,
    rstd,
    mean,
    xown,
    xhalo,
    a0,
    feat,
    a1,
    emb32,
    emb,
    eall,
    terms,
    factors,
    g,
    dsend,
    drecv,
    ssend,
    srecv,
    da1,
    da0,
    hsend,
    hrecv,
    hid_sem,
    in_sem,
    far_send,
    far_recv,
    emb_send,
    emb_recv,
    dem_send,
    dem_recv,
    sco_send,
    sco_recv,
):
    chunks, tokens, width = hid.shape
    full = chunks * width
    patch = head.shape[0]
    lanes = 2 * patch
    channels = up.shape[0]
    features_r = proj.shape[1]
    shard = fc1_t.shape[0]
    span = TPF // REGIONS
    rows = eall.shape[1]
    slices = eall.shape[0]
    spots = lax.axis_size("fsdp") // 2
    slots = 2 * SUB
    block = 16
    padded = cols.shape[0]

    ctx, fsdp = lax.axis_index("ctx"), lax.axis_index("fsdp")
    steps = lax.axis_size("ctx")
    z, core = fsdp // 2, fsdp % 2
    after = (lax.rem(ctx + 1, steps), fsdp)
    before = (lax.rem(ctx + steps - 1, steps), fsdp)
    twin = (ctx, z * 2 + 1 - core)
    side = 1 - 2 * lax.rem(z, 2)

    def other_core(offset):
        return (ctx, lax.rem(z + offset * side + spots, spots) * 2 + 1 - core)

    ups = [other_core(offset) for offset in (0, -1, 2, -3)]
    downs = [other_core(offset) for offset in (0, -1, -2, -3)]
    pair = (ctx, (z + side) * 2 + core)
    reach = [other_core(offset) for offset in (0, -1, -2, -3, 2)] + [pair]
    has_before, has_after = ctx > 0, ctx < steps - 1

    loads = []

    def load(source, target):
        copy = pltpu.make_async_copy(source, target, in_sem.at[len(loads)])
        copy.start()
        loads.append(copy)
        return copy

    load_proj = load(patch_proj, proj.at[pl.ds(0, channels)])
    load_cols = load(fc1_t, cols.at[pl.ds(0, shard)])
    load_mod = load(modulation, mod)
    load_head = load(head_weight, head)
    hid_loads = []
    for k in range(chunks):
        copy = pltpu.make_async_copy(
            hidden.at[:, pl.ds(k * width, width)], hid.at[k], hid_sem.at[k]
        )
        copy.start()
        hid_loads.append(copy)

    barrier = pltpu.get_barrier_semaphore()
    for peer in reach:
        pl.semaphore_signal(barrier, inc=1, device_id=peer, device_id_type=MESH)

    @pl.when(has_after)
    def _():
        pl.semaphore_signal(barrier, inc=1, device_id=after, device_id_type=MESH)

    @pl.when(has_before)
    def _():
        pl.semaphore_signal(barrier, inc=1, device_id=before, device_id_type=MESH)

    load_noisy = load(noisy_t, noisy)
    load_step = load(timestep_in, timestep)
    load_vec = load(reward_vec, vec_in)
    load_conv = []
    for frame in range(2):
        for lag in range(3):
            spot = frame + 2 - lag
            load_conv.append(
                load(
                    conv_weight.at[lag],
                    conv.at[pl.ds(spot * patch, patch), pl.ds(frame * channels, channels)],
                )
            )
    load_up = [
        load(up_weight.at[j], up.at[:, pl.ds(j * channels, channels)]) for j in range(SUB)
    ]

    proj[channels:, :] = jnp.ones((proj.shape[0] - channels, features_r), BF16)
    cols[shard:, :] = jnp.ones((padded - shard, features_r), BF16)
    vec[0] = jnp.zeros(vec.shape[1:], F32)

    @pl.when(jnp.logical_not(has_before))
    def _():
        xhalo[...] = jnp.zeros_like(xhalo)

    @pl.when(jnp.logical_not(has_after))
    def _():
        hrecv[...] = jnp.zeros_like(hrecv)

    empty = jnp.zeros((patch, channels), BF16)
    conv[0:patch, channels:] = empty
    conv[3 * patch :, :channels] = empty
    for k in range(chunks):
        wide[k, patch:, :] = jnp.ones((patch, width), BF16)

    def lane_at(shape):
        return lax.broadcasted_iota(jnp.int32, shape, 1)

    left = lane_at((TPF, lanes)) < patch
    row_id = lax.broadcasted_iota(jnp.int32, (lanes, lanes), 0)
    col_id = lane_at((lanes, lanes))
    to_left = jnp.where(col_id < patch, 1.0, 0.0).astype(BF16)
    to_right = jnp.where(col_id < patch, 0.0, 1.0).astype(BF16)
    each_half = jnp.where((row_id < patch) == (col_id < patch), 1.0, 0.0).astype(BF16)

    def prepare():
        for r in range(0, patch, block):
            part = slice(r, r + block)
            cs = jnp.zeros((block, lanes), F32)
            bw = jnp.zeros((block, lanes), F32)
            for c in range(0, full, lanes):
                columns = slice(c, c + lanes)
                plain = head[part, columns].astype(F32)
                scaled = (plain * (1.0 + mod[1:2, columns])).astype(BF16)
                wide[c // width, part, c % width : c % width + lanes] = scaled
                cs = cs + scaled.astype(F32)
                bw = bw + plain * mod[0:1, columns]
            sums_part[part, :], shift_part[part, :] = cs, bw

    def features(group):
        first = group[0] == 0
        product = dot_nt(hid[group[0]], wide[group[0]])
        for k in group[1:]:
            product = product + dot_nt(hid[k], wide[k])
        acc[...] = product if first else acc[...] + product
        for r in range(0, tokens, block):
            part = slice(r, r + block)
            centre = pilot[part, :]
            total = jnp.zeros((block, lanes), F32) if first else ssq[part, :]
            for k in group:
                for c in range(0, width, lanes):
                    value = hid[k, part, c : c + lanes].astype(F32) - centre
                    total = total + value * value
            ssq[part, :] = total

    def phase_mixed():
        product = dot_nt(proj[...], cols[...])
        centre = product[0:channels, shard : shard + 1] / features_r
        mixed[:, 0:padded] = jnp.where(
            lane_at((channels, padded)) < shard,
            product[0:channels, :] - centre * product[channels : channels + 1, :],
            0.0,
        ).astype(BF16)

    def phase_gram():
        gram = dot_nt(proj[...], proj[0:channels, :]) / features_r
        centre = jnp.sum(proj[0:channels, :].astype(F32), axis=1, keepdims=True) / features_r
        gram = gram[0:channels, :] - centre * gram[channels : channels + 1, :]
        high = gram.astype(BF16)
        mixed[:, 4 * padded : 4 * padded + channels] = high
        mixed[:, 4 * padded + channels :] = (gram - high.astype(F32)).astype(BF16)

    def column_sums(part):
        high = part.astype(BF16)
        rest = part - high.astype(F32)
        middle = rest.astype(BF16)
        low = (rest - middle.astype(F32)).astype(BF16)
        ones = jnp.ones((8, lanes), BF16)
        total = dot_nt(ones, jnp.concatenate([high, high], axis=0))
        total = total + dot_nt(ones, jnp.concatenate([middle, middle], axis=0))
        return (total + dot_nt(ones, jnp.concatenate([low, low], axis=0)))[0:1, :]

    load_proj.wait()
    load_cols.wait()
    phase_mixed()
    load_mod.wait()
    load_head.wait()
    prepare()
    head_sums = column_sums(sums_part[...])
    head_shift = column_sums(shift_part[...])
    hid_loads[0].wait()
    pilot[...] = jnp.broadcast_to(hid[0, :, 0:1].astype(F32), pilot.shape)
    groups = [[0]] + [list(range(k, min(k + 2, chunks))) for k in range(1, chunks, 2)]
    for group in groups:
        for k in group:
            if k > 0:
                hid_loads[k].wait()
        if group is groups[-1]:
            load_noisy.wait()
            twice = jnp.concatenate([noisy[...], noisy[...]], axis=0)
            token = lax.broadcasted_iota(jnp.int32, (TPF, 2 * TPF), 0)
            place = lane_at((TPF, 2 * TPF))
            latents[...] = jnp.where(
                left,
                dot_nt(jnp.where(token == place, 1.0, 0.0).astype(BF16), twice),
                dot_nt(jnp.where(token + TPF == place, 1.0, 0.0).astype(BF16), twice),
            )
        features(group)
    load_step.wait()
    step_frac = timestep[0:1, 0:lanes].astype(F32) / 1000.0
    sigma = 5.0 * step_frac / (1.0 + 4.0 * step_frac)

    reached = len(reach) + jnp.where(has_before, 1, 0) + jnp.where(has_after, 1, 0)
    pl.semaphore_wait(barrier, reached)

    def far(source, target, index, device):
        return pltpu.make_async_remote_copy(
            src_ref=source,
            dst_ref=target,
            send_sem=far_send.at[index],
            recv_sem=far_recv.at[index],
            device_id=device,
            device_id_type=MESH,
        )

    def share(index, source, target, device):
        moves = [
            far(
                mixed.at[:, pl.ds(source * padded, padded)],
                mixed.at[:, pl.ds(target * padded, padded)],
                index,
                device,
            ),
            far(vec.at[source], vec.at[target], index + 1, device),
        ]
        for move in moves:
            move.start()
        return moves

    load_vec.wait()
    vec[0, :, 0:shard] = jnp.broadcast_to(vec_in[...].astype(F32), (vec.shape[1], shard))
    share_pair = share(2, 0, 1, pair)
    share_twin = share(4, 0, 2, twin)

    def phase_latents():
        one, two = acc[0:TPF, :], acc[TPF:, :]
        average = jnp.where(left, pltpu.roll(one, patch, 1), two) / full
        product = jnp.where(left, one, pltpu.roll(two, patch, 1))
        off = average - jnp.where(left, pilot[0:TPF, :], pilot[TPF:, :])
        square = lane_sums(ssq[0:TPF, :], to_left) + lane_sums(ssq[TPF:, :], to_right)
        var = jnp.maximum(square / full - off * off, 0.0)
        scale = lax.rsqrt(var + EPSILON)
        mean[...] = average
        rstd[...] = scale
        velocity = scale * (product - average * head_sums)
        vel0[...] = velocity
        xown[...] = (latents[...] - sigma * (velocity + head_shift)).astype(BF16)

    phase_latents()

    move_x = far(xown, xhalo, 0, after)

    @pl.when(has_after)
    def _():
        move_x.start()

    phase_gram()
    for copy in load_conv + load_up:
        copy.wait()
    a0[...] = dot_nn(xown[...], conv[2 * patch :, :])

    @pl.when(has_before)
    def _():
        move_x.wait_recv()

    def phase_feat():
        a0[...] += dot_nn(xhalo[...], conv[0 : 2 * patch, :])
        for f in range(2):
            for r in range(0, TPF, block):
                value = a0[r : r + block, f * channels : (f + 1) * channels]
                feat[f * TPF + r : f * TPF + r + block, :] = silu(value).astype(BF16)

    phase_feat()

    def phase_upsample():
        for j in range(SUB):
            part = slice(j * channels, (j + 1) * channels)
            a1[:, part] = dot_nn(feat[...], up[:, part])
            for f in range(2):
                for p in range(REGIONS):
                    begin = f * TPF + p * span
                    pooled = jnp.sum(
                        silu(a1[begin : begin + span, part]), axis=0, keepdims=True
                    )
                    row = p * slots + f * SUB + j
                    emb32[row : row + 1, :] = pooled / span

    phase_upsample()
    emb[...] = emb32[...].astype(BF16)

    order = list(range(slices - 1, -1, -1))
    near, distant = [0, 1], [2, 3]
    line = near + distant

    move_emb = {}
    for d in order:
        move_emb[d] = pltpu.make_async_remote_copy(
            src_ref=emb,
            dst_ref=eall.at[d],
            send_sem=emb_send.at[d],
            recv_sem=emb_recv.at[d],
            device_id=ups[d],
            device_id_type=MESH,
        )
        move_emb[d].start()

    for move in share_pair:
        move.wait_recv()
    share_on = share(6, 1, 3, twin)

    def phase_slopes():
        for f in range(2):
            for r in range(0, TPF, block):
                for j in range(SUB):
                    part = slice(j * channels, (j + 1) * channels)
                    where = slice(f * TPF + r, f * TPF + r + block)
                    a1[where, part] = silu_slope(a1[where, part])
                part = slice(f * channels, (f + 1) * channels)
                a0[r : r + block, part] = silu_slope(a0[r : r + block, part])

    phase_slopes()
    for move in share_twin + share_on:
        move.wait_recv()
    weight = jnp.concatenate([vec[q] for q in range(4)], axis=1)[0:1, :]
    slot = lax.rem(lax.broadcasted_iota(jnp.int32, (rows, 1), 0), slots) + ctx * slots
    present = jnp.where((slot == 0) | (slot >= SUB), 1.0, 0.0)
    row_scale = present * (-LOSS_WEIGHT / REGIONS / span)

    def row_of(d):
        return line.index(d) * rows

    def all_rows(group):
        return slice(row_of(group[0]), row_of(group[-1]) + rows)

    def reward(group):
        part = all_rows(group)
        both = 4 * padded
        terms[part, :] = dot_nn(
            jnp.concatenate([eall[d] for d in group], axis=0), mixed[...]
        )
        coeff = 0.7978845608028654
        for d in group:
            total = None
            for r in range(0, rows, block):
                where = slice(row_of(d) + r, row_of(d) + r + block)
                pulled = terms[where, both : both + channels] + terms[where, both + channels :]
                own_emb = eall[d, r : r + block, :].astype(F32)
                var = jnp.sum(pulled * own_emb, axis=1, keepdims=True)
                scale = lax.rsqrt(jnp.maximum(var, 0.0) + EPSILON)
                value = terms[where, :both] * scale
                square = value * value
                tangent = jnp.tanh(value * (coeff + (coeff * 0.044715) * square))
                half = 0.5 * (1.0 + tangent)
                slope = half + 0.5 * value * (1.0 - tangent * tangent) * (
                    coeff + (coeff * 3.0 * 0.044715) * square
                )
                slope = (weight * slope).astype(BF16)
                g[where, :] = slope
                along = jnp.sum(slope.astype(F32) * value, axis=1, keepdims=True)
                factor = scale * row_scale[r : r + block]
                factors[where, :] = jnp.broadcast_to(factor, (block, 128))
                terms[where, both : both + channels] = pulled * (factor * scale * along)
                points = value * half * weight
                for q in range(0, block, slots):
                    for c in range(0, both, 128):
                        piece = points[q : q + slots, c : c + 128]
                        total = piece if total is None else total + piece
            ssend[d] = total

    def gradient(group):
        part = all_rows(group)
        both = 4 * padded
        back = dot_nt(g[part, :], mixed[:, 0:both])
        for d in group:
            where = slice(row_of(d), row_of(d) + rows)
            begin = row_of(d) - part.start
            dsend[d] = (
                back[begin : begin + rows] * factors[where, 0:1]
                - terms[where, both : both + channels]
            ).astype(BF16)

    move_dem, move_sco = {}, {}

    def send_back(group):
        for d in group:
            move_dem[d] = pltpu.make_async_remote_copy(
                src_ref=dsend.at[d],
                dst_ref=drecv.at[d],
                send_sem=dem_send.at[d],
                recv_sem=dem_recv.at[d],
                device_id=downs[d],
                device_id_type=MESH,
            )
            move_dem[d].start()

    for d in near:
        move_emb[d].wait_recv()

    def phase_near():
        reward(near)

    phase_near()
    for d in distant:
        move_emb[d].wait_recv()

    def phase_distant():
        reward(distant)
        gradient(distant)

    phase_distant()
    send_back(distant)

    def phase_nearback():
        gradient(near)

    phase_nearback()
    send_back(reversed(near))
    for d in order:
        move_sco[d] = pltpu.make_async_remote_copy(
            src_ref=ssend.at[d],
            dst_ref=srecv.at[d],
            send_sem=sco_send.at[d],
            recv_sem=sco_recv.at[d],
            device_id=downs[d],
            device_id_type=MESH,
        )
        move_sco[d].start()

    for d in order:
        move_dem[d].wait_recv()
    demb = drecv[0].astype(F32)
    for d in range(1, slices):
        demb = demb + drecv[d].astype(F32)
    emb32[...] = demb

    def phase_da0():
        for f in range(2):
            for j in range(SUB):
                part = slice(j * channels, (j + 1) * channels)
                spread = jnp.concatenate(
                    [
                        jnp.broadcast_to(
                            emb32[p * slots + f * SUB + j : p * slots + f * SUB + j + 1, :],
                            (span, channels),
                        )
                        for p in range(REGIONS)
                    ],
                    axis=0,
                )
                da1[f * TPF : (f + 1) * TPF, part] = (
                    spread * a1[f * TPF : (f + 1) * TPF, part]
                ).astype(BF16)
            dfeat = dot_nt(da1[f * TPF : (f + 1) * TPF, :], up[...])
            part = slice(f * channels, (f + 1) * channels)
            da0[:, part] = (dfeat * a0[:, part]).astype(BF16)

    phase_da0()

    def phase_hsend():
        hsend[...] = dot_nt(da0[...], conv[0 : 2 * patch, :]).astype(BF16)

    phase_hsend()
    move_h = far(hsend, hrecv, 1, before)

    @pl.when(has_before)
    def _():
        move_h.start()

    own = dot_nt(da0[...], conv[2 * patch :, :])

    for d in order:
        move_sco[d].wait_recv()
    total = srecv[0]
    for d in range(1, slices):
        total = total + srecv[d]
    total = jnp.sum(total, axis=1, keepdims=True) / REGIONS
    index = lax.broadcasted_iota(jnp.int32, (slots, 128), 0)
    where = index + ctx * slots
    keep = ((where == 0) | (where >= SUB)) & (index == lane_at((slots, 128)))
    reward_out[...] = jnp.sum(jnp.where(keep, total, 0.0), axis=0, keepdims=True)

    @pl.when(has_after)
    def _():
        move_h.wait_recv()

    def phase_final():
        grad = (-sigma) * (own + hrecv[...].astype(F32))
        lean = (rstd[...] * grad).astype(BF16).astype(F32)
        one = lane_sums(lean * head_sums, each_half) / full
        two = lane_sums(lean * vel0[...], each_half) / full
        slope = rstd[...] * two
        offset = slope * mean[...] - one
        high = offset.astype(BF16).astype(F32)
        middle = (offset - high).astype(BF16).astype(F32)
        low = offset - high - middle
        nth = lax.rem(lane_at((TPF, lanes)), patch)
        tail = jnp.where(nth == 0, high, jnp.where(nth == 1, middle, low))
        tail = jnp.where(nth < 3, tail, 0.0)
        other = pltpu.roll(slope, patch, 1)
        lhs_out[0:TPF, :] = jnp.where(left, lean, pltpu.roll(tail, patch, 1)).astype(BF16)
        lhs_out[TPF:, :] = jnp.where(left, pltpu.roll(lean, patch, 1), tail).astype(BF16)
        coef_out[0:TPF, :] = jnp.where(left, slope, other)
        coef_out[TPF:, :] = jnp.where(left, other, slope)

    phase_final()

    @pl.when(has_after)
    def _():
        move_x.wait_send()

    @pl.when(has_before)
    def _():
        move_h.wait_send()

    for move in share_pair + share_twin + share_on:
        move.wait_send()
    for d in order:
        move_emb[d].wait_send()
        move_dem[d].wait_send()
        move_sco[d].wait_send()


def tail_kernel(hid, wide, lhs, coef, rewards, grad, reward_out, held, sem):
    chunks, tokens, width = hid.shape
    lanes = coef.shape[1]
    piece = width // 2
    block = 16
    reward_out[...] = rewards[:, : reward_out.shape[1]]
    copies = []
    for k in range(chunks):
        for begin in range(0, width, piece):
            product = dot_nn(lhs[...], wide[k, :, begin : begin + piece])
            first = k * width + begin
            for r in range(0, tokens, block):
                part = slice(r, r + block)
                slope = coef[part, :]
                for c in range(0, piece, lanes):
                    value = hid[k, part, begin + c : begin + c + lanes].astype(F32)
                    held[part, first + c : first + c + lanes] = (
                        product[part, c : c + lanes] - value * slope
                    ).astype(BF16)
            columns = pl.ds(first, piece)
            copy = pltpu.make_async_copy(
                held.at[:, columns], grad.at[:, columns], sem.at[len(copies)]
            )
            copy.start()
            copies.append(copy)
    for copy in copies:
        copy.wait()


def per_device(
    hidden,
    modulation,
    head_weight,
    noisy,
    timestep,
    conv_weight,
    up_weight,
    patch_proj,
    fc1,
    reward_vec,
):
    states = hidden[0]
    tokens, full = states.shape
    patch = head_weight.shape[0]
    channels = up_weight.shape[1]
    features_r, shard = fc1.shape
    slices = 4
    rows = 2 * SUB * REGIONS
    slots = 2 * SUB
    lanes = 2 * patch
    width = 1024
    chunks = full // width
    padded = (shard // 128 + 1) * 128
    vmem = pltpu.VMEM

    scratch = [
        vmem((8, 128), jnp.int32),
        vmem((2, full), F32),
        vmem((patch, full), BF16),
        vmem((patch, tokens), BF16),
        vmem((4 * patch, 2 * channels), BF16),
        vmem((channels, SUB * channels), BF16),
        vmem((channels + 16, features_r), BF16),
        vmem((padded, features_r), BF16),
        vmem((channels, 4 * padded + 2 * channels), BF16),
        vmem((4, 8, padded), F32),
        vmem((1, shard), BF16),
        vmem((tokens, lanes), F32),
        vmem((tokens, lanes), F32),
        vmem((tokens, lanes), F32),
        vmem((patch, lanes), F32),
        vmem((patch, lanes), F32),
        vmem((TPF, lanes), F32),
        vmem((TPF, lanes), F32),
        vmem((TPF, lanes), F32),
        vmem((TPF, lanes), F32),
        vmem((TPF, lanes), BF16),
        vmem((TPF, lanes), BF16),
        vmem((TPF, 2 * channels), F32),
        vmem((tokens, channels), BF16),
        vmem((tokens, SUB * channels), F32),
        vmem((rows, channels), F32),
        vmem((rows, channels), BF16),
        vmem((slices, rows, channels), BF16),
        vmem((slices * rows, 4 * padded + 2 * channels), F32),
        vmem((slices * rows, 128), F32),
        vmem((slices * rows, 4 * padded), BF16),
        vmem((slices, rows, channels), BF16),
        vmem((slices, rows, channels), BF16),
        vmem((slices, slots, 128), F32),
        vmem((slices, slots, 128), F32),
        vmem((tokens, SUB * channels), BF16),
        vmem((TPF, 2 * channels), BF16),
        vmem((TPF, lanes), BF16),
        vmem((TPF, lanes), BF16),
        pltpu.SemaphoreType.DMA((chunks,)),
        pltpu.SemaphoreType.DMA((20,)),
        pltpu.SemaphoreType.DMA((8,)),
        pltpu.SemaphoreType.DMA((8,)),
        pltpu.SemaphoreType.DMA((slices,)),
        pltpu.SemaphoreType.DMA((slices,)),
        pltpu.SemaphoreType.DMA((slices,)),
        pltpu.SemaphoreType.DMA((slices,)),
        pltpu.SemaphoreType.DMA((slices,)),
        pltpu.SemaphoreType.DMA((slices,)),
    ]
    in_hbm = pl.BlockSpec(memory_space=pltpu.HBM)
    local = pl.BlockSpec(memory_space=pltpu.VMEM)
    hid, wide, lhs, coef, rewards = pl.pallas_call(
        main_kernel,
        out_shape=(
            vmem((chunks, tokens, width), BF16),
            vmem((chunks, lanes, width), BF16),
            vmem((tokens, lanes), BF16),
            vmem((tokens, lanes), F32),
            vmem((1, 128), F32),
        ),
        in_specs=[in_hbm] * 10,
        out_specs=(local,) * 5,
        scratch_shapes=scratch,
        compiler_params=pltpu.CompilerParams(
            collective_id=0, has_side_effects=True, vmem_limit_bytes=36 * 1024 * 1024
        ),
        name="reward_step",
    )(
        *(
            pltpu.with_memory_space_constraint(value, pltpu.HBM)
            for value in (
                jnp.broadcast_to(timestep, (8, 128)),
                states,
                modulation,
                head_weight,
                noisy[0].T,
                conv_weight,
                up_weight,
                patch_proj,
                fc1.T,
                reward_vec,
            )
        ),
    )
    grad, reward = pl.pallas_call(
        tail_kernel,
        out_shape=(
            jax.ShapeDtypeStruct((tokens, full), BF16),
            jax.ShapeDtypeStruct((1, slots), F32),
        ),
        in_specs=[local] * 5,
        out_specs=(in_hbm, local),
        scratch_shapes=[vmem((tokens, full), BF16), pltpu.SemaphoreType.DMA((2 * chunks,))],
        compiler_params=pltpu.CompilerParams(vmem_limit_bytes=20 * 1024 * 1024),
        name="hidden_gradient",
    )(hid, wide, lhs, coef, rewards)
    return (grad[None], reward)


def solution(mesh):
    return jax.shard_map(
        per_device,
        mesh=mesh,
        in_specs=(
            P("fsdp", "ctx", None),
            P(),
            P(),
            P("fsdp", "ctx", None),
            P(),
            P(),
            P(),
            P(),
            P(None, "fsdp"),
            P(None, "fsdp"),
        ),
        out_specs=(P("fsdp", "ctx", None), P("fsdp", "ctx")),
        check_vma=False,
    )
```

time: 141 us -> 40.3 us (0.29)
  the two profiles are of different devices: /device:TPU:24 before, /device:TPU:1 now
where the time goes in v2:
time: 40.3 us; the launch traced here: 40.2 us
  Pallas kernels  38.3 us (95%)
  between operations  1.28 us (3%)
  local copies, waits for them, and re-layouts  0.59 us (1%)
    pallas_call x1, Pallas kernels, per_device(): pl.pallas_call(main_kernel, out_shape=(vmem((chunks, tokens, width), BF16...  35.3 us
    pallas_call x1, Pallas kernels, per_device(): pl.pallas_call(tail_kernel, out_shape=(jax.ShapeDtypeStruct((tokens, full...  3 us

profile of v2, /device:TPU:1, one launch (start us, length us, event | category | flops | bytes accessed | tf_op | source)
XLA Modules:
  0.0 40.2 jit_solution(15257584002041884148)
XLA Ops:
  1.3 0.6 %broadcast_in_dim.8.timestep_in = s32[8,128]{1,0:T(8,128)} broadcast(s32[]{:T(128)} %bitcast.7), dimensions={} | broadcast | bytes 4100 | tf_op jit(solution)/shard_map/broadcast_in_dim | solution.py:757
  1.9 35.3 %reward_step.1 = (bf16[5,448,1024]{2,1,0:T(8,128)(2,1)S(1)}, bf16[5,128,1024]{2,1,0:T(8,128)(2,1)S(1)}, bf16[448,128]{1,0:T(8,128)(2,1)S(1)}, f32[448,128]{1,0:T(8,128)S(1)}, f32[1,128]{1,0:T(1,128)S(1)}) custom-call(s32[8,128]{1,0:T(8,128)} %broadcast_in_dim.8.timestep_in, bf16[448,5120]{1,0:T(8,128)(2,1)} %bitcast.8, f32[2,5120]{1,0:T(2,128)} %modulation.1, ...), custom_call_target="tpu_custom_call" | custom-call | tf_op jit(solution)/shard_map/reward_step/pallas_call | solution.py:737
  37.2 3.0 %hidden_gradient.1 = (bf16[448,5120]{1,0:T(8,128)(2,1)}, f32[1,8]{1,0:T(1,128)}) custom-call(bf16[5,448,1024]{2,1,0:T(8,128)(2,1)S(1)} %get-tuple-element.9.hid, bf16[5,128,1024]{2,1,0:T(8,128)(2,1)S(1)} %get-tuple-element.10.wide, bf16[448,128]{1,0:T(8,128)(2,1)S(1)} %get-tuple-element.11.lhs, f32[448,128]{1,0:T(8,128)S(1)} %get-tuple-element.12.coef, ...), custom_call_target="tpu_custom_call" | custom-call | tf_op jit(solution)/shard_map/hidden_gradient/pallas_call | solution.py:770

commit v3 on v2

--- a/solution.py
+++ b/solution.py
@@ -45,7 +45,7 @@
 
 
 def main_kernel(
-    timestep_in,
+    timestep,
     hidden,
     modulation,
     head_weight,
@@ -60,7 +60,6 @@
     lhs_out,
     coef_out,
     reward_out,
-    timestep,
     mod,
     head,
     noisy,
@@ -123,7 +122,6 @@
     spots = lax.axis_size("fsdp") // 2
     slots = 2 * SUB
     block = 16
-    padded = cols.shape[0]
 
     ctx, fsdp = lax.axis_index("ctx"), lax.axis_index("fsdp")
     steps = lax.axis_size("ctx")
@@ -175,7 +173,6 @@
         pl.semaphore_signal(barrier, inc=1, device_id=before, device_id_type=MESH)
 
     load_noisy = load(noisy_t, noisy)
-    load_step = load(timestep_in, timestep)
     load_vec = load(reward_vec, vec_in)
     load_conv = []
     for frame in range(2):
@@ -192,8 +189,7 @@
     ]
 
     proj[channels:, :] = jnp.ones((proj.shape[0] - channels, features_r), BF16)
-    cols[shard:, :] = jnp.ones((padded - shard, features_r), BF16)
-    vec[0] = jnp.zeros(vec.shape[1:], F32)
+    cols[shard:, :] = jnp.ones((cols.shape[0] - shard, features_r), BF16)
 
     @pl.when(jnp.logical_not(has_before))
     def _():
@@ -250,12 +246,10 @@
             ssq[part, :] = total
 
     def phase_mixed():
-        product = dot_nt(proj[...], cols[...])
-        centre = product[0:channels, shard : shard + 1] / features_r
-        mixed[:, 0:padded] = jnp.where(
-            lane_at((channels, padded)) < shard,
-            product[0:channels, :] - centre * product[channels : channels + 1, :],
-            0.0,
+        product = dot_nt(cols[...], proj[...])
+        centre = product[shard : shard + 1, 0:channels] / features_r
+        mixed[0:shard, :] = (
+            product[0:shard, 0:channels] - product[0:shard, channels : channels + 1] * centre
         ).astype(BF16)
 
     def phase_gram():
@@ -263,8 +257,8 @@
         centre = jnp.sum(proj[0:channels, :].astype(F32), axis=1, keepdims=True) / features_r
         gram = gram[0:channels, :] - centre * gram[channels : channels + 1, :]
         high = gram.astype(BF16)
-        mixed[:, 4 * padded : 4 * padded + channels] = high
-        mixed[:, 4 * padded + channels :] = (gram - high.astype(F32)).astype(BF16)
+        mixed[4 * shard : 4 * shard + channels, :] = high
+        mixed[4 * shard + channels :, :] = (gram - high.astype(F32)).astype(BF16)
 
     def column_sums(part):
         high = part.astype(BF16)
@@ -276,9 +270,35 @@
         total = total + dot_nt(ones, jnp.concatenate([middle, middle], axis=0))
         return (total + dot_nt(ones, jnp.concatenate([low, low], axis=0)))[0:1, :]
 
+    def far(source, target, index, device):
+        return pltpu.make_async_remote_copy(
+            src_ref=source,
+            dst_ref=target,
+            send_sem=far_send.at[index],
+            recv_sem=far_recv.at[index],
+            device_id=device,
+            device_id_type=MESH,
+        )
+
+    def share(index, source, target, device):
+        moves = [
+            far(
+                mixed.at[pl.ds(source * shard, shard)],
+                mixed.at[pl.ds(target * shard, shard)],
+                index,
+                device,
+            ),
+            far(vec.at[source], vec.at[target], index + 1, device),
+        ]
+        for move in moves:
+            move.start()
+        return moves
+
     load_proj.wait()
     load_cols.wait()
     phase_mixed()
+    load_vec.wait()
+    vec[0] = jnp.broadcast_to(vec_in[...].astype(F32), vec.shape[1:])
     load_mod.wait()
     load_head.wait()
     prepare()
@@ -302,41 +322,13 @@
                 dot_nt(jnp.where(token + TPF == place, 1.0, 0.0).astype(BF16), twice),
             )
         features(group)
-    load_step.wait()
-    step_frac = timestep[0:1, 0:lanes].astype(F32) / 1000.0
+        if group is groups[0]:
+            reached = len(reach) + jnp.where(has_before, 1, 0) + jnp.where(has_after, 1, 0)
+            pl.semaphore_wait(barrier, reached)
+            share_pair = share(2, 0, 1, pair)
+            share_twin = share(4, 0, 2, twin)
+    step_frac = jnp.full((1, lanes), timestep[0].astype(F32)) / 1000.0
     sigma = 5.0 * step_frac / (1.0 + 4.0 * step_frac)
-
-    reached = len(reach) + jnp.where(has_before, 1, 0) + jnp.where(has_after, 1, 0)
-    pl.semaphore_wait(barrier, reached)
-
-    def far(source, target, index, device):
-        return pltpu.make_async_remote_copy(
-            src_ref=source,
-            dst_ref=target,
-            send_sem=far_send.at[index],
-            recv_sem=far_recv.at[index],
-            device_id=device,
-            device_id_type=MESH,
-        )
-
-    def share(index, source, target, device):
-        moves = [
-            far(
-                mixed.at[:, pl.ds(source * padded, padded)],
-                mixed.at[:, pl.ds(target * padded, padded)],
-                index,
-                device,
-            ),
-            far(vec.at[source], vec.at[target], index + 1, device),
-        ]
-        for move in moves:
-            move.start()
-        return moves
-
-    load_vec.wait()
-    vec[0, :, 0:shard] = jnp.broadcast_to(vec_in[...].astype(F32), (vec.shape[1], shard))
-    share_pair = share(2, 0, 1, pair)
-    share_twin = share(4, 0, 2, twin)
 
     def phase_latents():
         one, two = acc[0:TPF, :], acc[TPF:, :]
@@ -440,8 +432,8 @@
 
     def reward(group):
         part = all_rows(group)
-        both = 4 * padded
-        terms[part, :] = dot_nn(
+        both = 4 * shard
+        terms[part, :] = dot_nt(
             jnp.concatenate([eall[d] for d in group], axis=0), mixed[...]
         )
         coeff = 0.7978845608028654
@@ -475,8 +467,8 @@
 
     def gradient(group):
         part = all_rows(group)
-        both = 4 * padded
-        back = dot_nt(g[part, :], mixed[:, 0:both])
+        both = 4 * shard
+        back = dot_nn(g[part, :], mixed[0:both, :])
         for d in group:
             where = slice(row_of(d), row_of(d) + rows)
             begin = row_of(d) - part.start
@@ -626,13 +618,14 @@
         move_sco[d].wait_send()
 
 
-def tail_kernel(hid, wide, lhs, coef, rewards, grad, reward_out, held, sem):
+def tail_kernel(hid, wide, lhs, coef, rewards, grad, reward_out, held, held_rewards, sem):
     chunks, tokens, width = hid.shape
     lanes = coef.shape[1]
     piece = width // 2
     block = 16
-    reward_out[...] = rewards[:, : reward_out.shape[1]]
-    copies = []
+    held_rewards[...] = rewards[:, : held_rewards.shape[1]]
+    copies = [pltpu.make_async_copy(held_rewards, reward_out, sem.at[0])]
+    copies[0].start()
     for k in range(chunks):
         for begin in range(0, width, piece):
             product = dot_nn(lhs[...], wide[k, :, begin : begin + piece])
@@ -678,20 +671,18 @@
     lanes = 2 * patch
     width = 1024
     chunks = full // width
-    padded = (shard // 128 + 1) * 128
     vmem = pltpu.VMEM
 
     scratch = [
-        vmem((8, 128), jnp.int32),
         vmem((2, full), F32),
         vmem((patch, full), BF16),
         vmem((patch, tokens), BF16),
         vmem((4 * patch, 2 * channels), BF16),
         vmem((channels, SUB * channels), BF16),
         vmem((channels + 16, features_r), BF16),
-        vmem((padded, features_r), BF16),
-        vmem((channels, 4 * padded + 2 * channels), BF16),
-        vmem((4, 8, padded), F32),
+        vmem((shard + 16, features_r), BF16),
+        vmem((4 * shard + 2 * channels, channels), BF16),
+        vmem((4, 8, shard), F32),
         vmem((1, shard), BF16),
         vmem((tokens, lanes), F32),
         vmem((tokens, lanes), F32),
@@ -710,9 +701,9 @@
         vmem((rows, channels), F32),
         vmem((rows, channels), BF16),
         vmem((slices, rows, channels), BF16),
-        vmem((slices * rows, 4 * padded + 2 * channels), F32),
+        vmem((slices * rows, 4 * shard + 2 * channels), F32),
         vmem((slices * rows, 128), F32),
-        vmem((slices * rows, 4 * padded), BF16),
+        vmem((slices * rows, 4 * shard), BF16),
         vmem((slices, rows, channels), BF16),
         vmem((slices, rows, channels), BF16),
         vmem((slices, slots, 128), F32),
@@ -743,7 +734,7 @@
             vmem((tokens, lanes), F32),
             vmem((1, 128), F32),
         ),
-        in_specs=[in_hbm] * 10,
+        in_specs=[pl.BlockSpec(memory_space=pltpu.SMEM)] + [in_hbm] * 9,
         out_specs=(local,) * 5,
         scratch_shapes=scratch,
         compiler_params=pltpu.CompilerParams(
@@ -751,10 +742,10 @@
         ),
         name="reward_step",
     )(
+        timestep,
         *(
             pltpu.with_memory_space_constraint(value, pltpu.HBM)
             for value in (
-                jnp.broadcast_to(timestep, (8, 128)),
                 states,
                 modulation,
                 head_weight,
@@ -774,8 +765,12 @@
             jax.ShapeDtypeStruct((1, slots), F32),
         ),
         in_specs=[local] * 5,
-        out_specs=(in_hbm, local),
-        scratch_shapes=[vmem((tokens, full), BF16), pltpu.SemaphoreType.DMA((2 * chunks,))],
+        out_specs=(in_hbm, in_hbm),
+        scratch_shapes=[
+            vmem((tokens, full), BF16),
+            vmem((1, slots), F32),
+            pltpu.SemaphoreType.DMA((2 * chunks + 1,)),
+        ],
         compiler_params=pltpu.CompilerParams(vmem_limit_bytes=20 * 1024 * 1024),
         name="hidden_gradient",
     )(hid, wide, lhs, coef, rewards)

time: 40.3 us -> 37 us (0.918)
  the two profiles are of different devices: /device:TPU:1 before, /device:TPU:24 now
where the time goes in v3:
time: 37 us; the launch traced here: 36.9 us
  Pallas kernels  35.7 us (96%)
  between operations  1.29 us (3%)
    pallas_call x1, Pallas kernels, per_device(): pl.pallas_call(main_kernel, out_shape=(vmem((chunks, tokens, width), BF16...  33.2 us
    pallas_call x1, Pallas kernels, per_device(): pl.pallas_call(tail_kernel, out_shape=(jax.ShapeDtypeStruct((tokens, full...  2.5 us

profile of v3, /device:TPU:24, one launch (start us, length us, event | category | flops | bytes accessed | tf_op | source)
XLA Modules:
  0.0 36.9 jit_solution(8204214723373693970)
XLA Ops:
  1.3 33.2 %reward_step.1 = (bf16[5,448,1024]{2,1,0:T(8,128)(2,1)S(1)}, bf16[5,128,1024]{2,1,0:T(8,128)(2,1)S(1)}, bf16[448,128]{1,0:T(8,128)(2,1)S(1)}, f32[448,128]{1,0:T(8,128)S(1)}, f32[1,128]{1,0:T(1,128)S(1)}) custom-call(s32[1]{0:T(128)S(6)} %copy.12.timestep, bf16[448,5120]{1,0:T(8,128)(2,1)} %bitcast.6, f32[2,5120]{1,0:T(2,128)} %modulation.1, ...), custom_call_target="tpu_custom_call" | custom-call | tf_op jit(solution)/shard_map/reward_step/pallas_call | solution.py:728
  34.4 2.5 %hidden_gradient.1 = (bf16[448,5120]{1,0:T(8,128)(2,1)}, f32[1,8]{1,0:T(1,128)}) custom-call(bf16[5,448,1024]{2,1,0:T(8,128)(2,1)S(1)} %get-tuple-element.9.hid, bf16[5,128,1024]{2,1,0:T(8,128)(2,1)S(1)} %get-tuple-element.10.wide, bf16[448,128]{1,0:T(8,128)(2,1)S(1)} %get-tuple-element.11.lhs, f32[448,128]{1,0:T(8,128)S(1)} %get-tuple-element.12.coef, ...), custom_call_target="tpu_custom_call" | custom-call | tf_op jit(solution)/shard_map/hidden_gradient/pallas_call | solution.py:761

commit v4 on v3

--- a/solution.py
+++ b/solution.py
@@ -38,10 +38,15 @@
     return (0.5 + 0.5 * tangent) * (1.0 + half * (1.0 - tangent))
 
 
-def lane_sums(value, pattern):
+def two_parts(value):
     high = value.astype(BF16)
-    low = (value - high.astype(F32)).astype(BF16)
-    return dot_nn(high, pattern) + dot_nn(low, pattern)
+    return [high, (value - high.astype(F32)).astype(BF16)]
+
+
+def lane_sums(values, patterns):
+    parts = [part for value in values for part in two_parts(value)]
+    rows = [pattern for pattern in patterns for _ in range(2)]
+    return dot_nn(jnp.concatenate(parts, axis=1), jnp.concatenate(rows, axis=0))
 
 
 def main_kernel(
@@ -131,11 +136,15 @@
     twin = (ctx, z * 2 + 1 - core)
     side = 1 - 2 * lax.rem(z, 2)
 
+    def chip(offset):
+        return lax.rem(z + offset * side + spots, spots)
+
     def other_core(offset):
-        return (ctx, lax.rem(z + offset * side + spots, spots) * 2 + 1 - core)
-
-    ups = [other_core(offset) for offset in (0, -1, 2, -3)]
-    downs = [other_core(offset) for offset in (0, -1, -2, -3)]
+        return (ctx, chip(offset) * 2 + 1 - core)
+
+    def turn(spot):
+        return jnp.where(spot >= spots // 2, 1, 0)
+
     pair = (ctx, (z + side) * 2 + core)
     reach = [other_core(offset) for offset in (0, -1, -2, -3, 2)] + [pair]
     has_before, has_after = ctx > 0, ctx < steps - 1
@@ -214,6 +223,7 @@
     to_left = jnp.where(col_id < patch, 1.0, 0.0).astype(BF16)
     to_right = jnp.where(col_id < patch, 0.0, 1.0).astype(BF16)
     each_half = jnp.where((row_id < patch) == (col_id < patch), 1.0, 0.0).astype(BF16)
+    nothing = jnp.zeros((lanes, lanes), BF16)
 
     def prepare():
         for r in range(0, patch, block):
@@ -247,28 +257,26 @@
 
     def phase_mixed():
         product = dot_nt(cols[...], proj[...])
-        centre = product[shard : shard + 1, 0:channels] / features_r
+        centre = product[shard : shard + 1, 0:channels] * (1.0 / features_r)
         mixed[0:shard, :] = (
             product[0:shard, 0:channels] - product[0:shard, channels : channels + 1] * centre
         ).astype(BF16)
 
     def phase_gram():
-        gram = dot_nt(proj[...], proj[0:channels, :]) / features_r
-        centre = jnp.sum(proj[0:channels, :].astype(F32), axis=1, keepdims=True) / features_r
-        gram = gram[0:channels, :] - centre * gram[channels : channels + 1, :]
+        product = dot_nt(proj[...], proj[...]) * (1.0 / features_r)
+        centre = product[0:channels, channels : channels + 1]
+        gram = product[0:channels, 0:channels] - centre * product[channels : channels + 1, 0:channels]
         high = gram.astype(BF16)
         mixed[4 * shard : 4 * shard + channels, :] = high
         mixed[4 * shard + channels :, :] = (gram - high.astype(F32)).astype(BF16)
 
-    def column_sums(part):
-        high = part.astype(BF16)
-        rest = part - high.astype(F32)
-        middle = rest.astype(BF16)
-        low = (rest - middle.astype(F32)).astype(BF16)
-        ones = jnp.ones((8, lanes), BF16)
-        total = dot_nt(ones, jnp.concatenate([high, high], axis=0))
-        total = total + dot_nt(ones, jnp.concatenate([middle, middle], axis=0))
-        return (total + dot_nt(ones, jnp.concatenate([low, low], axis=0)))[0:1, :]
+    def column_sums(values):
+        pieces = []
+        for value in values:
+            high, rest = two_parts(value)
+            low = (value - high.astype(F32) - rest.astype(F32)).astype(BF16)
+            pieces += [jnp.concatenate([high, rest, low], axis=1)] * 2
+        return dot_nt(jnp.ones((8, 3 * lanes), BF16), jnp.concatenate(pieces, axis=0))[0:1, :]
 
     def far(source, target, index, device):
         return pltpu.make_async_remote_copy(
@@ -302,8 +310,8 @@
     load_mod.wait()
     load_head.wait()
     prepare()
-    head_sums = column_sums(sums_part[...])
-    head_shift = column_sums(shift_part[...])
+    sums = column_sums([sums_part[...], shift_part[...]])
+    head_sums, head_shift = sums[:, 0:lanes], sums[:, lanes:]
     hid_loads[0].wait()
     pilot[...] = jnp.broadcast_to(hid[0, :, 0:1].astype(F32), pilot.shape)
     groups = [[0]] + [list(range(k, min(k + 2, chunks))) for k in range(1, chunks, 2)]
@@ -313,14 +321,12 @@
                 hid_loads[k].wait()
         if group is groups[-1]:
             load_noisy.wait()
-            twice = jnp.concatenate([noisy[...], noisy[...]], axis=0)
             token = lax.broadcasted_iota(jnp.int32, (TPF, 2 * TPF), 0)
             place = lane_at((TPF, 2 * TPF))
-            latents[...] = jnp.where(
-                left,
-                dot_nt(jnp.where(token == place, 1.0, 0.0).astype(BF16), twice),
-                dot_nt(jnp.where(token + TPF == place, 1.0, 0.0).astype(BF16), twice),
-            )
+            pick = jnp.concatenate([place == token, place == token + TPF], axis=0)
+            both = dot_nt(jnp.where(pick, 1.0, 0.0).astype(BF16), noisy[...])
+            pair_rows = jnp.concatenate([both[0:TPF], both[TPF:]], axis=1)
+            latents[...] = pair_rows
         features(group)
         if group is groups[0]:
             reached = len(reach) + jnp.where(has_before, 1, 0) + jnp.where(has_after, 1, 0)
@@ -332,11 +338,11 @@
 
     def phase_latents():
         one, two = acc[0:TPF, :], acc[TPF:, :]
-        average = jnp.where(left, pltpu.roll(one, patch, 1), two) / full
+        average = jnp.where(left, pltpu.roll(one, patch, 1), two) * (1.0 / full)
         product = jnp.where(left, one, pltpu.roll(two, patch, 1))
         off = average - jnp.where(left, pilot[0:TPF, :], pilot[TPF:, :])
-        square = lane_sums(ssq[0:TPF, :], to_left) + lane_sums(ssq[TPF:, :], to_right)
-        var = jnp.maximum(square / full - off * off, 0.0)
+        square = lane_sums([ssq[0:TPF, :], ssq[TPF:, :]], [to_left, to_right])
+        var = jnp.maximum(square * (1.0 / full) - off * off, 0.0)
         scale = lax.rsqrt(var + EPSILON)
         mean[...] = average
         rstd[...] = scale
@@ -381,26 +387,30 @@
                         silu(a1[begin : begin + span, part]), axis=0, keepdims=True
                     )
                     row = p * slots + f * SUB + j
-                    emb32[row : row + 1, :] = pooled / span
+                    emb32[row : row + 1, :] = pooled * (1.0 / span)
 
     phase_upsample()
     emb[...] = emb32[...].astype(BF16)
 
     order = list(range(slices - 1, -1, -1))
-    near, distant = [0, 1], [2, 3]
-    line = near + distant
-
-    move_emb = {}
-    for d in order:
-        move_emb[d] = pltpu.make_async_remote_copy(
+    line = list(range(slices))
+    first_half, second_half = line[:2], line[2:]
+
+    def send_emb(q, place, device):
+        return pltpu.make_async_remote_copy(
             src_ref=emb,
-            dst_ref=eall.at[d],
-            send_sem=emb_send.at[d],
-            recv_sem=emb_recv.at[d],
-            device_id=ups[d],
+            dst_ref=eall.at[place],
+            send_sem=emb_send.at[q],
+            recv_sem=emb_recv.at[place],
+            device_id=device,
             device_id_type=MESH,
         )
-        move_emb[d].start()
+
+    move_emb = {}
+    for q, offset in ((3, -3), (2, 2), (1, -1), (0, 0)):
+        place = lax.rem(q + turn(chip(offset)), slices)
+        move_emb[q] = send_emb(q, place, other_core(offset))
+        move_emb[q].start()
 
     for move in share_pair:
         move.wait_recv()
@@ -477,55 +487,48 @@
                 - terms[where, both : both + channels]
             ).astype(BF16)
 
-    move_dem, move_sco = {}, {}
-
-    def send_back(group):
-        for d in group:
-            move_dem[d] = pltpu.make_async_remote_copy(
-                src_ref=dsend.at[d],
-                dst_ref=drecv.at[d],
-                send_sem=dem_send.at[d],
-                recv_sem=dem_recv.at[d],
-                device_id=downs[d],
-                device_id_type=MESH,
-            )
-            move_dem[d].start()
-
-    for d in near:
-        move_emb[d].wait_recv()
-
-    def phase_near():
-        reward(near)
-
-    phase_near()
-    for d in distant:
-        move_emb[d].wait_recv()
-
-    def phase_distant():
-        reward(distant)
-        gradient(distant)
-
-    phase_distant()
-    send_back(distant)
-
-    def phase_nearback():
-        gradient(near)
-
-    phase_nearback()
-    send_back(reversed(near))
-    for d in order:
-        move_sco[d] = pltpu.make_async_remote_copy(
-            src_ref=ssend.at[d],
-            dst_ref=srecv.at[d],
-            send_sem=sco_send.at[d],
-            recv_sem=sco_recv.at[d],
-            device_id=downs[d],
+    def give_back(source, target, send_sem, recv_sem, p):
+        q = lax.rem(p + slices - turn(z), slices)
+        return pltpu.make_async_remote_copy(
+            src_ref=source.at[p],
+            dst_ref=target.at[q],
+            send_sem=send_sem.at[p],
+            recv_sem=recv_sem.at[q],
+            device_id=other_core(-q),
             device_id_type=MESH,
         )
-        move_sco[d].start()
-
-    for d in order:
-        move_dem[d].wait_recv()
+
+    def arrival(source, target, send_sem, recv_sem, q):
+        return pltpu.make_async_remote_copy(
+            src_ref=source.at[q],
+            dst_ref=target.at[q],
+            send_sem=send_sem.at[q],
+            recv_sem=recv_sem.at[q],
+            device_id=twin,
+            device_id_type=MESH,
+        )
+
+    back_refs = (dsend, drecv, dem_send, dem_recv)
+    score_refs = (ssend, srecv, sco_send, sco_recv)
+    move_dem, move_sco = {}, {}
+
+    def serve(group):
+        for p in group:
+            send_emb(0, p, twin).wait_recv()
+        reward(group)
+        gradient(group)
+        for p in group:
+            move_dem[p] = give_back(*back_refs, p)
+            move_dem[p].start()
+
+    serve(first_half)
+    serve(second_half)
+    for p in line:
+        move_sco[p] = give_back(*score_refs, p)
+        move_sco[p].start()
+
+    for q in line:
+        arrival(*back_refs, q).wait_recv()
     demb = drecv[0].astype(F32)
     for d in range(1, slices):
         demb = demb + drecv[d].astype(F32)
@@ -567,7 +570,7 @@
     own = dot_nt(da0[...], conv[2 * patch :, :])
 
     for d in order:
-        move_sco[d].wait_recv()
+        arrival(*score_refs, d).wait_recv()
     total = srecv[0]
     for d in range(1, slices):
         total = total + srecv[d]
@@ -584,9 +587,15 @@
     def phase_final():
         grad = (-sigma) * (own + hrecv[...].astype(F32))
         lean = (rstd[...] * grad).astype(BF16).astype(F32)
-        one = lane_sums(lean * head_sums, each_half) / full
-        two = lane_sums(lean * vel0[...], each_half) / full
-        slope = rstd[...] * two
+        means = lane_sums(
+            [lean * head_sums, lean * vel0[...]],
+            [
+                jnp.concatenate([each_half, nothing], axis=1),
+                jnp.concatenate([nothing, each_half], axis=1),
+            ],
+        ) * (1.0 / full)
+        one = means[:, 0:lanes]
+        slope = rstd[...] * means[:, lanes:]
         offset = slope * mean[...] - one
         high = offset.astype(BF16).astype(F32)
         middle = (offset - high).astype(BF16).astype(F32)

time: 37 us -> 36.5 us (0.986); the launches traced: 36.9 us -> 36 us
  Pallas kernels: 35.7 us -> 34.7 us
    pallas_call x1, Pallas kernels: 33.2 us -> 32.2 us  [per_device(): pl.pallas_call(main_kernel, out_shape=(vmem((chunks, tokens, width), BF16...]
where the time goes in v4:
time: 36.5 us; the launch traced here: 36 us
  Pallas kernels  34.7 us (95%)
  between operations  1.29 us (4%)
    pallas_call x1, Pallas kernels, per_device(): pl.pallas_call(main_kernel, out_shape=(vmem((chunks, tokens, width), BF16...  32.2 us
    pallas_call x1, Pallas kernels, per_device(): pl.pallas_call(tail_kernel, out_shape=(jax.ShapeDtypeStruct((tokens, full...  2.5 us

profile of v4, /device:TPU:24, one launch (start us, length us, event | category | flops | bytes accessed | tf_op | source)
XLA Modules:
  0.0 36.0 jit_solution(4910355664372953180)
XLA Ops:
  1.3 32.2 %reward_step.1 = (bf16[5,448,1024]{2,1,0:T(8,128)(2,1)S(1)}, bf16[5,128,1024]{2,1,0:T(8,128)(2,1)S(1)}, bf16[448,128]{1,0:T(8,128)(2,1)S(1)}, f32[448,128]{1,0:T(8,128)S(1)}, f32[1,128]{1,0:T(1,128)S(1)}) custom-call(s32[1]{0:T(128)S(6)} %copy.12.timestep, bf16[448,5120]{1,0:T(8,128)(2,1)} %bitcast.6, f32[2,5120]{1,0:T(2,128)} %modulation.1, ...), custom_call_target="tpu_custom_call" | custom-call | tf_op jit(solution)/shard_map/reward_step/pallas_call | solution.py:737
  33.5 2.5 %hidden_gradient.1 = (bf16[448,5120]{1,0:T(8,128)(2,1)}, f32[1,8]{1,0:T(1,128)}) custom-call(bf16[5,448,1024]{2,1,0:T(8,128)(2,1)S(1)} %get-tuple-element.9.hid, bf16[5,128,1024]{2,1,0:T(8,128)(2,1)S(1)} %get-tuple-element.10.wide, bf16[448,128]{1,0:T(8,128)(2,1)S(1)} %get-tuple-element.11.lhs, f32[448,128]{1,0:T(8,128)S(1)} %get-tuple-element.12.coef, ...), custom_call_target="tpu_custom_call" | custom-call | tf_op jit(solution)/shard_map/hidden_gradient/pallas_call | solution.py:770

commit v5 on v4

--- a/solution.py
+++ b/solution.py
@@ -157,8 +157,6 @@
         loads.append(copy)
         return copy
 
-    load_proj = load(patch_proj, proj.at[pl.ds(0, channels)])
-    load_cols = load(fc1_t, cols.at[pl.ds(0, shard)])
     load_mod = load(modulation, mod)
     load_head = load(head_weight, head)
     hid_loads = []
@@ -168,6 +166,8 @@
         )
         copy.start()
         hid_loads.append(copy)
+    load_proj = load(patch_proj, proj.at[pl.ds(0, channels)])
+    load_cols = load(fc1_t, cols.at[pl.ds(0, shard)])
 
     barrier = pltpu.get_barrier_semaphore()
     for peer in reach:
@@ -302,11 +302,6 @@
             move.start()
         return moves
 
-    load_proj.wait()
-    load_cols.wait()
-    phase_mixed()
-    load_vec.wait()
-    vec[0] = jnp.broadcast_to(vec_in[...].astype(F32), vec.shape[1:])
     load_mod.wait()
     load_head.wait()
     prepare()
@@ -328,7 +323,12 @@
             pair_rows = jnp.concatenate([both[0:TPF], both[TPF:]], axis=1)
             latents[...] = pair_rows
         features(group)
-        if group is groups[0]:
+        if group is groups[1]:
+            load_proj.wait()
+            load_cols.wait()
+            phase_mixed()
+            load_vec.wait()
+            vec[0] = jnp.broadcast_to(vec_in[...].astype(F32), vec.shape[1:])
             reached = len(reach) + jnp.where(has_before, 1, 0) + jnp.where(has_after, 1, 0)
             pl.semaphore_wait(barrier, reached)
             share_pair = share(2, 0, 1, pair)

time: 36.5 us -> 35.6 us (0.975)
  Pallas kernels: 34.7 us -> 34 us
    pallas_call x1, Pallas kernels: 32.2 us -> 31.5 us  [per_device(): pl.pallas_call(main_kernel, out_shape=(vmem((chunks, tokens, width), BF16...]
where the time goes in v5:
time: 35.6 us; the launch traced here: 35.3 us
  Pallas kernels  34 us (96%)
  between operations  1.29 us (4%)
    pallas_call x1, Pallas kernels, per_device(): pl.pallas_call(main_kernel, out_shape=(vmem((chunks, tokens, width), BF16...  31.5 us
    pallas_call x1, Pallas kernels, per_device(): pl.pallas_call(tail_kernel, out_shape=(jax.ShapeDtypeStruct((tokens, full...  2.5 us

profile of v5, /device:TPU:24, one launch (start us, length us, event | category | flops | bytes accessed | tf_op | source)
XLA Modules:
  0.0 35.3 jit_solution(18333679613795563956)
XLA Ops:
  1.3 31.5 %reward_step.1 = (bf16[5,448,1024]{2,1,0:T(8,128)(2,1)S(1)}, bf16[5,128,1024]{2,1,0:T(8,128)(2,1)S(1)}, bf16[448,128]{1,0:T(8,128)(2,1)S(1)}, f32[448,128]{1,0:T(8,128)S(1)}, f32[1,128]{1,0:T(1,128)S(1)}) custom-call(s32[1]{0:T(128)S(6)} %copy.12.timestep, bf16[448,5120]{1,0:T(8,128)(2,1)} %bitcast.6, f32[2,5120]{1,0:T(2,128)} %modulation.1, ...), custom_call_target="tpu_custom_call" | custom-call | tf_op jit(solution)/shard_map/reward_step/pallas_call | solution.py:737
  32.8 2.5 %hidden_gradient.1 = (bf16[448,5120]{1,0:T(8,128)(2,1)}, f32[1,8]{1,0:T(1,128)}) custom-call(bf16[5,448,1024]{2,1,0:T(8,128)(2,1)S(1)} %get-tuple-element.9.hid, bf16[5,128,1024]{2,1,0:T(8,128)(2,1)S(1)} %get-tuple-element.10.wide, bf16[448,128]{1,0:T(8,128)(2,1)S(1)} %get-tuple-element.11.lhs, f32[448,128]{1,0:T(8,128)S(1)} %get-tuple-element.12.coef, ...), custom_call_target="tpu_custom_call" | custom-call | tf_op jit(solution)/shard_map/hidden_gradient/pallas_call | solution.py:770
